TPU v7x, 32 devices: a whole 2x2x4 slice. The times are simulated.
32 devices in a mesh: leaf: 32 (over z, y, x, core).
Axes of the slice: x: 2, y: 2, z: 4, core: 2. Of those that a mesh axis runs over, the one named last changes fastest.
Arguments:
- leaf_bases: float32 [1024, 64, 128], P('leaf'), may hold values from -0.6 to 0.6
- transfers: float32 [512, 64, 128], P('leaf'), may hold values from -0.5 to 0.5
- leaf_blocks: float32 [64, 64, 8192], P(None, None, 'leaf'), may hold values from -6 to 6
- parent_blocks: float32 [64, 64, 8192], P(None, None, 'leaf'), may hold values from -6 to 6
- leaf_rows: int32 [8192], P('leaf'), may hold values from 0 to 31
- leaf_slots: int32 [8192], P('leaf'), may hold values from 0 to 127, as said below
- leaf_requests: int32 [32, 128], P('leaf'), may hold values from 0 to 31
- parent_rows: int32 [8192], P('leaf'), may hold values from 0 to 15
- parent_slots: int32 [8192], P('leaf'), may hold values from 0 to 127, as said below
- parent_requests: int32 [32, 128], P('leaf'), may hold values from 0 to 15
- block_counts: int32 [32, 2], P('leaf'), may hold values from 160 to 256, as said below
Outputs:
- leaf_basis: float32 [1024, 64, 128], P('leaf')
- new_transfers: float32 [512, 64, 128], P('leaf')
- leaf_coupling: float32 [64, 64, 8192], P(None, None, 'leaf')
- parent_coupling: float32 [64, 64, 8192], P(None, None, 'leaf')
Inputs may be any that keep to these rules, and one draw needn't show every extreme that they name: `leaf_slots`: slot s names a cluster of device s // 4; several blocks of a device may name one slot, and every slot is named by some block of each device. `parent_slots`: slot s names a cluster of device s // 4; several blocks of a device may name one slot, and every slot is named by some block of each device. `block_counts`: column 0 lies in 160 to 256, column 1 in 160 to 256; live blocks are the first ones of a device.
All inputs are finite; a program needn't handle non-finite values.
Results may differ from a plain program's by a relative error of at most 0.0003.
Values sent between devices are 32-bit elements; how exact they have to be, the bound alone decides.
No kernel may reach another device: no remote copies, remote signals or barrier semaphores. Data moves between devices by JAX's collectives and lax.ppermute only.
A program may use at most 192 MiB of HBM per device.

v0:
```python
import jax
import jax.numpy as jnp
from jax import lax
from jax.sharding import PartitionSpec as P

PRECISE = lax.Precision.HIGHEST


def leaf_factors(leaf_bases):
    leaf_gram = jnp.einsum("lkp,ljp->lkj", leaf_bases, leaf_bases, precision=PRECISE)
    leaf_lower = jnp.linalg.cholesky(leaf_gram)
    leaf_basis = jax.scipy.linalg.solve_triangular(leaf_lower, leaf_bases, lower=True)
    return (leaf_lower, leaf_basis)


def parent_merge(leaf_lower, transfers):
    parent_total = transfers.shape[0]
    rank_dim = transfers.shape[1]
    child_upper = jnp.swapaxes(leaf_lower, 1, 2).reshape(parent_total, 2, rank_dim, rank_dim)
    child_pieces = transfers.reshape(parent_total, rank_dim, 2, rank_dim)
    stacked = jnp.einsum("pcik,pkcj->pcij", child_upper, child_pieces, precision=PRECISE)
    parent_gram = jnp.einsum("pcki,pckj->pij", stacked, stacked, precision=PRECISE)
    parent_lower = jnp.linalg.cholesky(parent_gram)
    wide_lower = jnp.broadcast_to(parent_lower[:, None], (parent_total, 2, rank_dim, rank_dim))
    solved = jax.scipy.linalg.solve_triangular(wide_lower, jnp.swapaxes(stacked, 2, 3), lower=True)
    new_transfers = jnp.transpose(solved, (0, 3, 1, 2)).reshape(
        parent_total, rank_dim, 2 * rank_dim
    )
    return (new_transfers, parent_lower)


def project_rows(table, rows, blocks):
    row_factors = jnp.take(table, rows, axis=2)
    return jnp.einsum("ikb,kjb->ijb", row_factors, blocks, precision=PRECISE)


def mask_blocks(coupled, block_total):
    live_mask = jnp.arange(coupled.shape[2], dtype=jnp.int32) < block_total
    return jnp.where(live_mask[None, None, :], coupled, jnp.zeros_like(coupled))


def close_blocks(left_products, fetched, slots, block_total):
    rank_dim = left_products.shape[0]
    column_factors = jnp.take(fetched.reshape(rank_dim, rank_dim, -1), slots, axis=2)
    coupled = jnp.einsum("ijb,ljb->ilb", left_products, column_factors, precision=PRECISE)
    return mask_blocks(coupled, block_total)


def fetch_leaf(table, wanted):

    def serve_rows(wanted_here):
        fetched = jnp.take(table, wanted_here, axis=2)
        return lax.all_to_all(fetched, "leaf", split_axis=2, concat_axis=2, tiled=True)

    return serve_rows(lax.all_to_all(wanted, "leaf", split_axis=0, concat_axis=0, tiled=True))


def fetch_parent(table, wanted):

    def serve_rows(wanted_here):
        fetched = jnp.take(table, wanted_here, axis=2)
        return lax.all_to_all(fetched, "leaf", split_axis=2, concat_axis=2, tiled=True)

    return serve_rows(lax.all_to_all(wanted, "leaf", split_axis=0, concat_axis=0, tiled=True))


def per_device(
    leaf_bases,
    transfers,
    leaf_blocks,
    parent_blocks,
    leaf_rows,
    leaf_slots,
    leaf_requests,
    parent_rows,
    parent_slots,
    parent_requests,
    block_counts,
):
    leaf_lower, leaf_basis = leaf_factors(leaf_bases)
    new_transfers, parent_lower = parent_merge(leaf_lower, transfers)
    leaf_table = jnp.transpose(leaf_lower, (2, 1, 0))
    parent_table = jnp.transpose(parent_lower, (2, 1, 0))
    peer_count = lax.axis_size("leaf")
    leaf_wanted = leaf_requests[0].reshape(peer_count, -1)
    parent_wanted = parent_requests[0].reshape(peer_count, -1)
    leaf_total = block_counts[0, 0]
    parent_total = block_counts[0, 1]
    leaf_left = project_rows(leaf_table, leaf_rows, leaf_blocks)
    parent_left = project_rows(parent_table, parent_rows, parent_blocks)
    leaf_far = fetch_leaf(leaf_table, leaf_wanted)
    parent_far = fetch_parent(parent_table, parent_wanted)
    leaf_coupling = close_blocks(leaf_left, leaf_far, leaf_slots, leaf_total)
    parent_coupling = close_blocks(parent_left, parent_far, parent_slots, parent_total)
    return (leaf_basis, new_transfers, leaf_coupling, parent_coupling)


def solution(mesh):
    in_specs = (
        P("leaf", None, None),
        P("leaf", None, None),
        P(None, None, "leaf"),
        P(None, None, "leaf"),
        P("leaf"),
        P("leaf"),
        P("leaf", None),
        P("leaf"),
        P("leaf"),
        P("leaf", None),
        P("leaf", None),
    )
    out_specs = (
        P("leaf", None, None),
        P("leaf", None, None),
        P(None, None, "leaf"),
        P(None, None, "leaf"),
    )
    return jax.shard_map(
        per_device, mesh=mesh, in_specs=in_specs, out_specs=out_specs, check_vma=False
    )
```

profile of v0, /device:TPU:0, one launch (start us, length us, event | category | flops | bytes accessed | tf_op | source)
XLA Modules:
  0.0 779.8 jit_solution(12151904331484465711)
XLA Ops:
  1.2 1.2 reduce.18
  3.1 7.3 all-to-all-start
  10.4 1.8 fusion.45
  12.5 1.1 fusion.34
  13.7 189.1 %custom-call.16 = f32[32,64,64]{2,1,0:T(8,128)} custom-call(f32[32,64,64]{2,1,0:T(8,128)} %fusion.34), custom_call_target="Cholesky" | custom-call | tf_op jit(solution)/shard_map/jit(cholesky)/cholesky | solution.py:11
  202.8 1.9 copy.91
  205.4 3.2 fusion.30
  208.6 2.9 copy.94
  211.5 2.6 reshape.146
  214.2 2.9 copy.104
  218.4 5.8 all-to-all-start.2
  224.7 2.8 gather_fusion
  227.5 4.6 fusion.43
  232.1 5.4 reshape.225
  237.5 6.1 all-to-all-start.1
  243.7 2.4 fusion.35
  246.1 1.0 copy-done.1
  247.1 2.0 convolution_bitcast_fusion
  250.1 94.5 %custom-call.18 = f32[16,64,64]{2,1,0:T(8,128)S(1)} custom-call(f32[16,64,64]{2,1,0:T(8,128)} %fusion.37), custom_call_target="Cholesky" | custom-call | tf_op jit(solution)/shard_map/jit(cholesky)/cholesky | solution.py:23
  344.9 1.1 broadcast_select_fusion
  346.0 158.7 %custom-call.19 = f32[16,2,1,64,64]{3,4,2,1,0:T(8,128)} custom-call(f32[16,2,1,64,64]{4,3,2,1,0:T(8,128)} %broadcast_select_fusion), custom_call_target="InvertDiagBlocksLowerTriangular" | custom-call | tf_op jit(solution)/shard_map/jit(_solve_triangular)/vmap(vmap())/triangular_solve | solution.py:25
  504.9 4.4 fusion.32
  509.6 2.8 gather_fusion.2
  512.4 5.6 copy.114
  518.1 4.6 fusion.44
  522.7 5.5 reshape.227
  528.1 6.3 all-to-all-start.3
  534.4 68.4 %custom-call.17 = f32[32,1,64,64]{0,2,3,1:T(8,128)} custom-call(f32[32,1,64,64]{0,3,2,1:T(8,128)} %get-tuple-element.23), custom_call_target="InvertDiagBlocksLowerTriangular" | custom-call | tf_op jit(solution)/shard_map/jit(_solve_triangular)/vmap()/triangular_solve | solution.py:12
  602.9 3.9 copy.93
  606.8 2.3 copy.117
  609.1 9.2 %copy.108 = f32[64,64,256]{1,0,2:T(8,128)} copy(f32[64,64,256]{2,1,0:T(8,128)} %param.15) | data formatting | bytes 8388608 | tf_op args[2]
  618.3 4.3 gather_fusion.1
  622.6 9.0 %copy.106 = f32[256,64,64]{1,2,0:T(8,128)} copy(f32[256,64,64]{2,1,0:T(8,128)} %gather_fusion.1) | data formatting | bytes 8388608 | tf_op jit(solution)/shard_map/jit(_take)/gather | solution.py:33
  631.6 9.2 %copy.116 = f32[64,64,256]{1,0,2:T(8,128)} copy(f32[64,64,256]{2,1,0:T(8,128)} %param.16) | data formatting | bytes 8388608 | tf_op args[3]
  640.8 4.3 gather_fusion.3
  647.1 2.1 fusion.46
  649.3 20.8 %fusion.7 = f32[256,64,64]{2,1,0:T(8,128)} fusion(f32[64,64,256]{1,0,2:T(8,128)} %copy.108, f32[256,64,64]{1,2,0:T(8,128)} %copy.106, pred[256]{0:T(512)(128)(4,1)S(1)} %compare_and_fusion.4), kind=kOutput, calls=%fused_computation.13 | convolution fusion | flops 806354944 | bytes 12583168 | tf_op jit(solution)/shard_map/ikb,kjb->ijb/dot_general | solution.py:34
  670.0 17.3 %fusion.2 = f32[256,64,64]{2,1,0:T(8,128)} fusion(f32[64,64,256]{1,0,2:T(8,128)S(1)} %bitcast.108, f32[256,64,64]{1,2,0:T(8,128)S(1)} %bitcast.110, pred[256]{0:T(512)(128)(4,1)S(1)} %compare_and_fusion.2), kind=kOutput, calls=%fused_computation.8 | convolution fusion | flops 806354944 | bytes 12583168 | tf_op jit(solution)/shard_map/ikb,kjb->ijb/dot_general | solution.py:34
  687.8 7.3 reduce.20
  695.1 3.0 reshape.226
  698.1 6.5 gather_fusion.4
  704.6 20.1 %select_bitcast_fusion.1 = f32[64,64,256]{0,1,2:T(8,128)} fusion(pred[256]{0:T(512)(128)(4,1)S(1)} %get-tuple-element.27, f32[256,64,64]{2,1,0:T(8,128)} %fusion.7, f32[256,64,64]{2,1,0:T(8,128)} %gather_fusion.4, pred[256]{0:T(512)(128)(4,1)S(1)} %get-tuple-element.26), kind=kOutput, calls=%fused_computation.21 | convolution fusion | flops 807403520 | bytes 12583424 | tf_op jit(solution)/shard_map/ijb,ljb->ilb/dot_general | solution.py:45
  724.8 8.8 %copy.118 = f32[64,64,256]{2,1,0:T(8,128)} copy(f32[64,64,256]{0,1,2:T(8,128)} %select_bitcast_fusion.1) | data formatting | bytes 8388608
  733.6 7.3 reduce.21
  740.9 3.0 reshape.228
  743.9 6.5 gather_fusion.5
  750.4 20.3 %select_bitcast_fusion = f32[64,64,256]{0,1,2:T(8,128)} fusion(pred[256]{0:T(512)(128)(4,1)S(1)} %get-tuple-element.29, f32[256,64,64]{2,1,0:T(8,128)} %fusion.2, f32[256,64,64]{2,1,0:T(8,128)} %gather_fusion.5, pred[256]{0:T(512)(128)(4,1)S(1)} %get-tuple-element.28), kind=kOutput, calls=%fused_computation.20 | convolution fusion | flops 807403520 | bytes 12583424 | tf_op jit(solution)/shard_map/ijb,ljb->ilb/dot_general | solution.py:45
  770.7 8.6 %copy.119 = f32[64,64,256]{2,1,0:T(8,128)} copy(f32[64,64,256]{0,1,2:T(8,128)} %select_bitcast_fusion) | data formatting | bytes 8388608
  (74 shorter events, 8.4 us)
Async XLA Ops:
  0.6 9.8 %copy-start = (f32[32,64,128]{2,1,0:T(8,128)S(1)}, f32[32,64,128]{2,1,0:T(8,128)}, u32[]{:S(2)}) copy-start(f32[32,64,128]{2,1,0:T(8,128)} %param.13) | copy-start | bytes 3145732
  3.1 215.3 %all-to-all-start = ((s32[32,1,4]{2,1,0:T(1,128)}), s32[32,1,4]{2,1,0:T(1,128)S(1)}, u32[]{:S(2)}, u32[]{:S(2)}) async-start(s32[32,1,4]{2,1,0:T(1,128)} %bitcast.12), calls=%async_computation | async-start | bytes 32768 | tf_op jit(solution)/shard_map/all_to_all | solution.py:55
  205.3 11.8 %copy-start.8 = (s32[1,128]{1,0:T(1,128)S(1)}, s32[1,128]{1,0:T(1,128)}, u32[]{:S(2)}) copy-start(s32[1,128]{1,0:T(1,128)} %param.22) | copy-start | bytes 1540
  218.4 19.1 %all-to-all-start.2 = ((s32[32,1,4]{2,1,0:T(1,128)}), s32[32,1,4]{2,1,0:T(1,128)S(1)}, u32[]{:S(2)}, u32[]{:S(2)}) async-start(s32[32,1,4]{2,1,0:T(1,128)} %bitcast.24), calls=%async_computation.2 | async-start | bytes 32768 | tf_op jit(solution)/shard_map/all_to_all | solution.py:64
  237.5 267.2 %copy-start.6 = (s32[256]{0:T(256)S(1)}, s32[256]{0:T(256)}, u32[]{:S(2)}) copy-start(s32[256]{0:T(256)} %param.17) | copy-start | bytes 3076
  237.5 267.2 %copy-start.3 = (s32[256]{0:T(256)S(1)}, s32[256]{0:T(256)}, u32[]{:S(2)}) copy-start(s32[256]{0:T(256)} %param.18) | copy-start | bytes 3076
  237.5 267.2 %copy-start.7 = (s32[256]{0:T(256)S(1)}, s32[256]{0:T(256)}, u32[]{:S(2)}) copy-start(s32[256]{0:T(256)} %param.20) | copy-start | bytes 3076
  237.5 267.2 %copy-start.4 = (s32[256]{0:T(256)S(1)}, s32[256]{0:T(256)}, u32[]{:S(2)}) copy-start(s32[256]{0:T(256)} %param.21) | copy-start | bytes 3076
  237.5 290.6 %all-to-all-start.1 = ((f32[32,1,16384]{2,1,0:T(1,128)}), f32[32,1,16384]{2,1,0:T(1,128)}, u32[]{:S(2)}, u32[]{:S(2)}) async-start(f32[32,1,16384]{2,1,0:T(1,128)} %reshape.225), calls=%async_computation.1 | async-start | bytes 4194304 | tf_op jit(solution)/shard_map/all_to_all | solution.py:53
  246.1 1.0 copy-start.1
  528.1 205.5 %all-to-all-start.3 = ((f32[32,1,16384]{2,1,0:T(1,128)}), f32[32,1,16384]{2,1,0:T(1,128)}, u32[]{:S(2)}, u32[]{:S(2)}) async-start(f32[32,1,16384]{2,1,0:T(1,128)} %reshape.227), calls=%async_computation.3 | async-start | bytes 4194304 | tf_op jit(solution)/shard_map/all_to_all | solution.py:62
  631.6 13.6 %copy-start.5 = (s32[1,2]{1,0:T(1,128)S(1)}, s32[1,2]{1,0:T(1,128)}, u32[]{:S(2)}) copy-start(s32[1,2]{1,0:T(1,128)} %param.23) | copy-start | bytes 28
  631.6 15.5 %copy-start.2 = (f32[32,64,64]{2,1,0:T(8,128)S(1)}, f32[32,64,64]{2,1,0:T(8,128)}, u32[]{:S(2)}) copy-start(f32[32,64,64]{2,1,0:T(8,128)} %copy.93) | copy-start | bytes 1572868
  647.1 22.9 %slice-start = ((s8[8388608]{0:T(1024)(128)(4,1)}), s8[4194304]{0:T(1024)(128)(4,1)S(1)}, s32[]{:S(2)}) async-start(s8[8388608]{0:T(1024)(128)(4,1)} %bitcast.107), calls=%async_computation.4 | async-start | bytes 8388608
  647.1 22.9 %slice-start.2 = ((s8[8388608]{0:T(1024)(128)(4,1)}), s8[4194304]{0:T(1024)(128)(4,1)S(1)}, s32[]{:S(2)}) async-start(s8[8388608]{0:T(1024)(128)(4,1)} %bitcast.109), calls=%async_computation.6 | async-start | bytes 8388608
  649.3 20.8 %slice-start.1 = ((s8[8388608]{0:T(1024)(128)(4,1)}), s8[4194304]{0:T(1024)(128)(4,1)S(1)}, s32[]{:S(2)}) async-start(s8[8388608]{0:T(1024)(128)(4,1)} %bitcast.107), calls=%async_computation.5 | async-start | bytes 8388608
  649.3 20.8 %slice-start.3 = ((s8[8388608]{0:T(1024)(128)(4,1)}), s8[4194304]{0:T(1024)(128)(4,1)S(1)}, s32[]{:S(2)}) async-start(s8[8388608]{0:T(1024)(128)(4,1)} %bitcast.109), calls=%async_computation.7 | async-start | bytes 8388608
where the time goes:
time: 789 us; the launch traced here: 780 us
  other arithmetic  545 us (69%)
  local copies, waits for them, and re-layouts  117 us (15%)
  matrix products  91.1 us (12%)
  starting transfers between devices  25.6 us (3%)
    another operation x4, other arithmetic, leaf_factors(): leaf_lower = jnp.linalg.cholesky(leaf_gram)  190 us
    another operation x2, other arithmetic, parent_merge(): jax.scipy.linalg.solve_triangular(wide_lower, jnp.swapaxes(stacked, 2, 3)...  160 us
    another operation x3, other arithmetic, parent_merge(): parent_lower = jnp.linalg.cholesky(parent_gram)  94.7 us
    another operation x2, other arithmetic, leaf_factors(): jax.scipy.linalg.solve_triangular(leaf_lower, leaf_bases, lower=True)  68.4 us
    unnamed x36, local copies, waits for them, and re-layouts  56.6 us
    dot_general x2, matrix products, close_blocks(): jnp.einsum('ijb,ljb->ilb', left_products, column_factors, precision=PRECISE)  40.4 us
    dot_general x2, matrix products, project_rows(): return jnp.einsum('ikb,kjb->ijb', row_factors, blocks, precision=PRECISE)  38 us
    gather x3, local copies, waits for them, and re-layouts, project_rows(): row_factors = jnp.take(table, rows, axis=2)  17.6 us
  transfers between devices with their start and end apart: 4, of which 0 were waited for; matrix products, arithmetic and copies ran while one was open for 90% of the time, Pallas kernels for 0%

commit v1 on v0

v1 whole, which is shorter than its diff:
```python
import functools

import jax
import jax.numpy as jnp
from jax import lax
from jax.experimental import pallas as pl
from jax.experimental.pallas import tpu as pltpu
from jax.sharding import PartitionSpec as P

F32=jnp.float32; BF16=jnp.bfloat16
HI=lax.Precision.HIGHEST
NT=(((1,),(1,)),((),()))
NN=(((1,),(0,)),((),()))

def seg_tiles(k, tiles):
    p, s = divmod(k, 8)
    low = [(8*(tiles-p)+s, jv) for jv in range(tiles-p, tiles)] if p else []
    return low + [(k, jv) for jv in range(p, tiles)]

def chunk_tiles(e):
    if e < 16:
        return seg_tiles(e, 8) + seg_tiles(e+16, 8)
    return [(32 + 4*(e-16) + s, jv) for s in (1, 0, 3, 2) for jv in range(4, 8)]

def split(x):
    hi = x.astype(BF16)
    return hi, (x - hi.astype(F32)).astype(BF16)

def factor_kernel(u_ref, e_ref, table_ref, r_ref, rinv_ref, nat, gd, a_ref):
    L = u_ref.shape[0]; Pn = e_ref.shape[0]; C = L+Pn
    lane = lax.broadcasted_iota(jnp.int32, (64,128), 1)
    left = lane < 64
    left32 = left[:32]
    def gram(l, c):
        u = u_ref[l]
        g = lax.dot_general(u, jnp.concatenate([u,u],0), NT, precision=HI, preferred_element_type=F32)
        gd[l] = g
        nat[pl.ds(l*32,32),:] = jnp.where(left32, g[:32], g[32:])
        return c
    lax.fori_loop(0, L, gram, 0, unroll=4)
    def parent(p, c):
        e = e_ref[p]
        er = pltpu.roll(e, 64, 1)
        e0 = jnp.where(left, e, er); e1 = jnp.where(left, er, e)
        t0 = lax.dot_general(gd[2*p][:, :64], e0, NN, precision=HI, preferred_element_type=F32)
        t1 = lax.dot_general(gd[2*p+1][:, :64], e1, NN, precision=HI, preferred_element_type=F32)
        est = jnp.concatenate([e0,e1],0).T[:64]
        g = lax.dot_general(est, jnp.concatenate([t0,t1],0), NN, precision=HI, preferred_element_type=F32)
        nat[pl.ds((L+p)*32,32),:] = jnp.where(left32, g[:32], g[32:])
        return c
    lax.fori_loop(0, Pn, parent, 0, unroll=4)
    zeros = jnp.zeros((128-C,128), F32)
    for i in range(32):
        x = jnp.concatenate([nat[pl.ds(i, C, 32), :], zeros], 0).T
        a_ref[i] = x[:64]
        a_ref[i+32] = x[64:]
    live = lax.broadcasted_iota(jnp.int32, (1,128), 1) < C
    sub = lax.broadcasted_iota(jnp.int32, (8,128), 0)
    for p in range(8):
        b = 8*p
        T = [a_ref[b+kk, b:b+8, :] for kk in range(8)]
        for kk in range(8):
            inv = lax.rsqrt(jnp.where(live, T[kk][kk:kk+1,:], 1.0))
            row = jnp.where(sub >= kk, T[kk]*inv, 0.0)
            rinv_ref[pl.ds(b+kk,1), :] = inv
            r_ref[b+kk, b:b+8, :] = row
            for k2 in range(kk+1, 8):
                T[k2] = T[k2] - row[k2:k2+1,:]*row
        for q in range(p+1, 8):
            T = []
            for kk in range(8):
                s = a_ref[b+kk, 8*q:8*q+8, :]
                for t in range(kk):
                    s = s - r_ref[b+t, pl.ds(b+kk,1), :]*T[t]
                T.append(s*rinv_ref[pl.ds(b+kk,1), :])
                r_ref[b+kk, 8*q:8*q+8, :] = T[kk]
        for q in range(p+1, 8):
            def upd(h, c):
                i0 = 8*q + 4*h
                acc = [[a_ref[i0+u, 8*j:8*j+8, :] for j in range(q,8)] for u in range(4)]
                for kk in range(8):
                    v = [r_ref[b+kk, 8*j:8*j+8, :] for j in range(q,8)]
                    for u in range(4):
                        m = r_ref[b+kk, pl.ds(i0+u,1), :]
                        for j in range(8-q):
                            acc[u][j] = acc[u][j] - m*v[j]
                for u in range(4):
                    for j in range(q,8):
                        a_ref[i0+u, 8*j:8*j+8, :] = acc[u][j-q]
                return c
            lax.fori_loop(0, 2, upd, 0, unroll=True)
    row = lax.broadcasted_iota(jnp.int32, (C,128), 0)
    col = lax.broadcasted_iota(jnp.int32, (C,128), 1)
    eye = (row == col).astype(F32).astype(BF16)
    eye2 = jnp.concatenate([eye, eye], 1)
    for e in range(18):
        ch = jnp.concatenate([r_ref[k, 8*j:8*j+8, :] for k, j in chunk_tiles(e)], 0)
        hi, lo = split(ch)
        table_ref[e] = lax.dot_general(eye2, jnp.concatenate([hi,lo],1), NT, preferred_element_type=F32)

def factor(u, e):
    L, Pn = u.shape[0], e.shape[0]; C = L+Pn
    return pl.pallas_call(factor_kernel,
        out_shape=(jax.ShapeDtypeStruct((18,C,128),F32), jax.ShapeDtypeStruct((64,64,128),F32), jax.ShapeDtypeStruct((64,128),F32)),
        scratch_shapes=[pltpu.VMEM((C*32,128),F32), pltpu.VMEM((L,64,128),F32), pltpu.VMEM((64,64,128),F32)],
        compiler_params=pltpu.CompilerParams(vmem_limit_bytes=40*2**20),
        name="factor")(u, e)

def unpack(v):
    lane = lax.broadcasted_iota(jnp.int32, (8,128), 1)
    sub = lax.broadcasted_iota(jnp.int32, (8,128), 0)
    half = lane & 63
    left = lane < 64
    v0, v1 = v[0:8], v[8:16]
    w0, w1 = pltpu.roll(v0, 64, 1), pltpu.roll(v1, 64, 1)
    y = jnp.where(sub < 4, v[16:17], v[17:18])
    z = pltpu.roll(pltpu.roll(y, 0, 1, stride=16, stride_axis=0), 0, 1, stride=16, stride_axis=0)
    parts = [
        jnp.where(left, v0, w0),
        jnp.where(left, v1, w1),
        jnp.where(left, w0, v0),
        jnp.where(left, w1, v1),
        jnp.where(left, z, pltpu.roll(z, 64, 1)),
        jnp.where(left, pltpu.roll(v1, 104, 1), pltpu.roll(v1, 40, 1)),
        jnp.where(left, pltpu.roll(v0, 112, 1), pltpu.roll(v0, 48, 1)),
        jnp.where(left, pltpu.roll(v1, 56, 1), pltpu.roll(v1, 120, 1)),
    ]
    return jnp.concatenate([x if p == 0 else jnp.where(half >= 8*p, x, 0.0) for p, x in enumerate(parts)], 0)

def mix(x):
    left = lax.broadcasted_iota(jnp.int32, x.shape, 1) < 64
    hi = x.astype(BF16).astype(F32)
    return jnp.where(left, hi, x - hi).astype(BF16)

def left_kernel(base, clusters, total, rows_ref, table_ref, s_ref, out_ref, m_ref, lhs_ref):
    h = pl.program_id(0)
    @pl.when(h == 0)
    def _():
        def prep(c, _):
            lhs_ref[c] = mix(unpack(table_ref[pl.ds(base + c, 18, total), :]))
            return _
        lax.fori_loop(0, clusters, prep, 0, unroll=4)
    for k in range(32):
        m_ref[pl.ds(k, 128, 32), :] = jnp.concatenate([s_ref[k], s_ref[k+32]], 0).T
    left = lax.broadcasted_iota(jnp.int32, (32,128), 1) < 64
    def one(b, _):
        m = m_ref[pl.ds(pl.multiple_of(b*32, 32), 32), :]
        t = pltpu.roll(m, 64, 1)
        hi, lo = split(jnp.concatenate([jnp.where(left, m, t), jnp.where(left, t, m)], 0))
        a = lhs_ref[rows_ref[h*128 + b]]
        res = lax.dot_general(jnp.concatenate([a, a], 1), jnp.concatenate([hi,hi,lo,lo], 0), NN, preferred_element_type=F32)
        out_ref[b] = mix(res)
        return _
    lax.fori_loop(0, 128, one, 0, unroll=8)

def left_products(rows, table, blocks, base, clusters):
    total = table.shape[0]//18
    B = blocks.shape[2]
    return pl.pallas_call(functools.partial(left_kernel, base, clusters, total),
        grid=(B//128,),
        in_specs=[pl.BlockSpec(memory_space=pltpu.SMEM), pl.BlockSpec(table.shape, lambda h: (0,0)),
                  pl.BlockSpec((64,64,128), lambda h: (0,0,h))],
        out_specs=pl.BlockSpec((128,64,128), lambda h: (h,0,0)),
        out_shape=jax.ShapeDtypeStruct((B,64,128), BF16),
        scratch_shapes=[pltpu.VMEM((128*32,128),F32), pltpu.VMEM((clusters,64,128),BF16)],
        compiler_params=pltpu.CompilerParams(vmem_limit_bytes=40*2**20), name="left")(rows, table, blocks)

def close_kernel(cap, offset, wide, slots_ref, count_ref, p_ref, f_ref, out_ref, c_ref, w_ref):
    h = pl.program_id(0)
    peers = f_ref.shape[0]//(18*wide)
    @pl.when(h == 0)
    def _():
        def prep(n, _):
            for t in range(cap):
                hi, lo = split(unpack(f_ref[pl.ds(n*18*wide + offset + t, 18, wide), :]))
                w_ref[n*cap + t] = jnp.concatenate([hi, lo], 1)
            return _
        lax.fori_loop(0, peers, prep, 0, unroll=max(1, 4//cap))
    def one(b, _):
        a = p_ref[b]
        res = lax.dot_general(jnp.concatenate([a, a], 1), w_ref[slots_ref[h*128 + b]], NT, preferred_element_type=F32)
        c_ref[pl.ds(pl.multiple_of(b*32, 32), 32), :] = jnp.concatenate([res[:32], res[32:]], 1)
        return _
    lax.fori_loop(0, 128, one, 0, unroll=8)
    live = lax.broadcasted_iota(jnp.int32, (64,128), 1) + h*128 < count_ref[0]
    for i in range(32):
        x = c_ref[pl.ds(i, 128, 32), :].T
        out_ref[i] = jnp.where(live, x[:64], 0.0)
        out_ref[i+32] = jnp.where(live, x[64:], 0.0)

def close(slots, count, prods, fetched, cap, offset, wide):
    B = prods.shape[0]
    S = fetched.shape[0]//(18*wide)*cap
    return pl.pallas_call(functools.partial(close_kernel, cap, offset, wide),
        grid=(B//128,),
        in_specs=[pl.BlockSpec(memory_space=pltpu.SMEM), pl.BlockSpec(memory_space=pltpu.SMEM),
                  pl.BlockSpec((128,64,128), lambda h: (h,0,0)), pl.BlockSpec(fetched.shape, lambda h: (0,0))],
        out_specs=pl.BlockSpec((64,64,128), lambda h: (0,0,h)),
        out_shape=jax.ShapeDtypeStruct((64,64,B), F32),
        scratch_shapes=[pltpu.VMEM((128*32,128),F32), pltpu.VMEM((S,64,256),BF16)],
        compiler_params=pltpu.CompilerParams(vmem_limit_bytes=48*2**20), name="close")(slots, count, prods, fetched)

def gather_kernel(idx_ref, table_ref, out_ref):
    C = table_ref.shape[1]; S = idx_ref.shape[1]
    pad = jnp.zeros((128-C, 128), F32)
    hot = (lax.broadcasted_iota(jnp.int32, (128,S), 0) == idx_ref[...]).astype(F32).T.astype(BF16)
    hot = jnp.concatenate([hot, hot], 1)
    for e in range(18):
        hi, lo = split(jnp.concatenate([table_ref[e], pad], 0))
        res = lax.dot_general(hot, jnp.concatenate([hi, lo], 0), NN, preferred_element_type=F32)
        if out_ref.ndim == 4:
            out_ref[:, e] = res.reshape(out_ref.shape[0], 8, 128)
        else:
            out_ref[e] = res

def gather(idx, table):
    n, wide = idx.shape
    direct = wide == 8
    shape = (n,18,wide,128) if direct else (18,n*wide,128)
    out = pl.pallas_call(gather_kernel, out_shape=jax.ShapeDtypeStruct(shape,F32),
        compiler_params=pltpu.CompilerParams(vmem_limit_bytes=32*2**20), name="gather")(idx.reshape(1,-1), table)
    return out if direct else out.reshape(18,n,wide,128).transpose(1,0,2,3)

def basis_kernel(u_ref, e_ref, table_ref, r_ref, rinv_ref, basis_ref, nt_ref, x_ref, nat):
    L = u_ref.shape[0]; Pn = e_ref.shape[0]; C = L+Pn
    sub = lax.broadcasted_iota(jnp.int32, (8,128), 0)
    zero = jnp.zeros((8,128), F32)
    for q in range(8):
        def rows(h, _):
            acc = [[zero]*q for u in range(4)]
            for t in range(8*q):
                v = [x_ref[t, 8*j:8*j+8, :] for j in range(t//8+1)]
                for u in range(4):
                    m = r_ref[t, pl.ds(8*q+4*h+u,1), :]
                    for j in range(t//8+1):
                        acc[u][j] = acc[u][j] - m*v[j]
            for u in range(4):
                for j in range(q):
                    x_ref[8*q+4*h+u, 8*j:8*j+8, :] = acc[u][j]
            return _
        if q:
            lax.fori_loop(0, 2, rows, 0, unroll=True)
        for j in range(q+1):
            T = []
            for u in range(8):
                s = (sub == u).astype(F32) if j == q else x_ref[8*q+u, 8*j:8*j+8, :]
                for t in range(u):
                    s = s - r_ref[8*q+t, pl.ds(8*q+u,1), :]*T[t]
                T.append(s*rinv_ref[pl.ds(8*q+u,1), :])
                x_ref[8*q+u, 8*j:8*j+8, :] = T[u]
        for j in range(q+1, 8):
            for u in range(8):
                x_ref[8*q+u, 8*j:8*j+8, :] = zero
    for i in range(32):
        nat[pl.ds(i, C, 32), :] = jnp.concatenate([x_ref[i], x_ref[i+32]], 0).T[:C]
    left32 = lax.broadcasted_iota(jnp.int32, (32,128), 1) < 64
    left = lax.broadcasted_iota(jnp.int32, (64,128), 1) < 64
    def inverse(c):
        m = nat[pl.ds(c*32,32),:]
        t = pltpu.roll(m, 64, 1)
        return jnp.concatenate([jnp.where(left32, m, t), jnp.where(left32, t, m)], 0)[:, :64]
    def leaf(l, _):
        basis_ref[l] = lax.dot_general(inverse(l), u_ref[l], NN, precision=HI, preferred_element_type=F32)
        return _
    lax.fori_loop(0, L, leaf, 0, unroll=4)
    def parent(p, _):
        e = e_ref[p]
        er = pltpu.roll(e, 64, 1)
        est = jnp.concatenate([jnp.where(left, e, er), jnp.where(left, er, e)],0).T[:64]
        w = lax.dot_general(inverse(L+p), est, NN, precision=HI, preferred_element_type=F32)
        wr = pltpu.roll(w, 64, 1)
        r0 = unpack(table_ref[pl.ds(2*p, 18, C), :])[:, :64]
        r1 = unpack(table_ref[pl.ds(2*p+1, 18, C), :])[:, :64]
        n0 = lax.dot_general(r0, jnp.concatenate([w,w],0)[:, :64], NT, precision=HI, preferred_element_type=F32)
        n1 = lax.dot_general(r1, jnp.concatenate([wr,wr],0)[:, :64], NT, precision=HI, preferred_element_type=F32)
        nt_ref[p] = jnp.where(left, n0, n1)
        return _
    lax.fori_loop(0, Pn, parent, 0, unroll=4)

def bases(u, e, table, r, rinv):
    C = u.shape[0]+e.shape[0]
    return pl.pallas_call(basis_kernel,
        out_shape=(jax.ShapeDtypeStruct(u.shape,F32), jax.ShapeDtypeStruct(e.shape,F32)),
        scratch_shapes=[pltpu.VMEM((64,64,128),F32), pltpu.VMEM((C*32,128),F32)],
        compiler_params=pltpu.CompilerParams(vmem_limit_bytes=40*2**20), name="basis")(u, e, table, r, rinv)

def per_device(
    leaf_bases, transfers, leaf_blocks, parent_blocks, leaf_rows, leaf_slots, leaf_requests,
    parent_rows, parent_slots, parent_requests, block_counts,
):
    leaves = leaf_bases.shape[0]
    parents = transfers.shape[0]
    peers = lax.axis_size("leaf")
    cap = leaf_requests.shape[1] // peers
    pcap = parent_requests.shape[1] // peers
    wide = cap + pcap
    wanted = jnp.concatenate(
        [leaf_requests[0].reshape(peers, cap), leaves + parent_requests[0].reshape(peers, pcap)], 1
    )
    wanted_here = lax.all_to_all(wanted, "leaf", 0, 0, tiled=True)
    table, r, rinv = factor(leaf_bases, transfers)
    sent = gather(wanted_here, table)
    fetched = lax.all_to_all(sent, "leaf", 0, 0, tiled=True).reshape(-1, 128)
    flat = table.reshape(-1, 128)
    leaf_left = left_products(leaf_rows, flat, leaf_blocks, 0, leaves)
    parent_left = left_products(parent_rows, flat, parent_blocks, leaves, parents)
    leaf_basis, new_transfers = bases(leaf_bases, transfers, flat, r, rinv)
    leaf_coupling = close(leaf_slots, block_counts[0, :1], leaf_left, fetched, cap, 0, wide)
    parent_coupling = close(parent_slots, block_counts[0, 1:], parent_left, fetched, pcap, cap, wide)
    return (leaf_basis, new_transfers, leaf_coupling, parent_coupling)


def solution(mesh):
    rows = P("leaf", None, None)
    blocks = P(None, None, "leaf")
    ids = P("leaf")
    per_owner = P("leaf", None)
    return jax.shard_map(
        per_device,
        mesh=mesh,
        in_specs=(rows, rows, blocks, blocks, ids, ids, per_owner, ids, ids, per_owner, per_owner),
        out_specs=(rows, rows, blocks, blocks),
        check_vma=False,
    )
```

time: 789 us -> 136 us (0.17); the launches traced: 780 us -> 135 us
  other arithmetic: 545 us -> 3.37 us
  Pallas kernels: 0 us -> 102 us
  local copies, waits for them, and re-layouts: 117 us -> 15.3 us
  matrix products: 91.1 us -> 0 us
  starting transfers between devices: 25.6 us -> 13.3 us
    another operation x11 -> x0, other arithmetic: 513 us -> none  [the longest x4 190 us: leaf_factors(): leaf_lower = jnp.linalg.cholesky(leaf_gram)]
    pallas_call x0 -> x7, Pallas kernels: none -> 102 us  [the longest x2 44.3 us: close(): pl.pallas_call(functools.partial(close_kernel, cap, offset, wide), grid=(...]
    dot_general x7 -> x0, matrix products: 84.6 us -> none  [the longest x2 40.4 us: close_blocks(): jnp.einsum('ijb,ljb->ilb', left_products, column_factors, precision=PRECISE)]
    unnamed x36 -> x33, local copies, waits for them, and re-layouts: 56.6 us -> 14.5 us
    gather x8 -> x0, local copies, waits for them, and re-layouts: 41.9 us -> none  [the longest x3 17.6 us: project_rows(): row_factors = jnp.take(table, rows, axis=2)]
    all_to_all x2 -> x1, other arithmetic: 14.6 us -> 0.69 us  [per_device(): wanted_here = lax.all_to_all(wanted, 'leaf', 0, 0, tiled=True)]
    all_to_all x4 -> x2, starting transfers between devices: 25.6 us -> 13.3 us  [the longest x1 7.3 us: per_device(): wanted_here = lax.all_to_all(wanted, 'leaf', 0, 0, tiled=True)]
    unnamed x6 -> x1, other arithmetic: 10.9 us -> 1.32 us
  transfers between devices with their start and end apart: 4 -> 2, of which waited for: 0 -> 0; matrix products, arithmetic and copies ran while one was open for 90% -> 0% of each run, Pallas kernels for 0% -> 42%
where the time goes in v1:
time: 136 us; the launch traced here: 135 us
  Pallas kernels  102 us (75%)
  local copies, waits for them, and re-layouts  15.3 us (11%)
  starting transfers between devices  13.3 us (10%)
  other arithmetic  3.37 us (2%)
    pallas_call x2, Pallas kernels, close(): pl.pallas_call(functools.partial(close_kernel, cap, offset, wide), grid=(...  44.3 us
    pallas_call x2, Pallas kernels, left_products(): pl.pallas_call(functools.partial(left_kernel, base, clusters, total), gri...  29.6 us
    pallas_call x1, Pallas kernels, bases(): pl.pallas_call(basis_kernel, out_shape=(jax.ShapeDtypeStruct(u.shape, F32...  16.2 us
    unnamed x33, local copies, waits for them, and re-layouts  14.5 us
    pallas_call x1, Pallas kernels, factor(): pl.pallas_call(factor_kernel, out_shape=(jax.ShapeDtypeStruct((18, C, 128...  11.6 us
    all_to_all x1, starting transfers between devices, per_device(): wanted_here = lax.all_to_all(wanted, 'leaf', 0, 0, tiled=True)  7.3 us
    all_to_all x1, starting transfers between devices, per_device(): fetched = lax.all_to_all(sent, 'leaf', 0, 0, tiled=True).reshape(-1, 128)  6.01 us
  transfers between devices with their start and end apart: 2, of which 0 were waited for; matrix products, arithmetic and copies ran while one was open for 0% of the time, Pallas kernels for 42%

profile of v1, /device:TPU:0, one launch (start us, length us, event | category | flops | bytes accessed | tf_op | source)
XLA Modules:
  0.0 135.3 jit_solution(17830911038102218539)
XLA Ops:
  0.6 0.7 add_reduce_fusion
  1.3 0.1 add.11
  1.4 0.5 broadcast.11
  1.9 1.3 reduce.10
  3.2 0.1 reshape_squeeze.4
  3.3 0.7 pad_add_fusion
  4.0 7.3 %all-to-all-start = ((s32[32,1,8]{2,1,0:T(1,128)}), s32[32,1,8]{2,1,0:T(1,128)S(1)}, u32[]{:S(2)}, u32[]{:S(2)}) async-start(s32[32,1,8]{2,1,0:T(1,128)} %bitcast.3), calls=%async_computation | async-start | bytes 32768 | tf_op jit(solution)/shard_map/all_to_all | solution.py:300
  11.3 0.0 copy-start.5
  11.4 1.2 copy-done.5
  12.6 0.0 copy-start.9
  12.6 1.0 copy-done.9
  13.6 0.0 copy-start.10
  13.6 11.6 %factor.1 = (f32[18,48,128]{2,1,0:T(8,128)S(1)}, f32[64,64,128]{2,1,0:T(8,128)S(1)}, f32[64,128]{1,0:T(8,128)S(1)}) custom-call(f32[32,64,128]{2,1,0:T(8,128)S(1)} %copy-done.5, f32[16,64,128]{2,1,0:T(8,128)S(1)} %copy-done.9), custom_call_target="tpu_custom_call" | custom-call | tf_op jit(solution)/shard_map/factor/pallas_call | solution.py:103
  25.2 0.0 copy-start.7
  25.2 1.3 copy-done.7
  26.5 0.0 all-to-all-done
  26.5 0.7 reduce.11
  27.2 0.1 reshape.23.idx_ref
  27.3 0.8 gather.1
  28.1 0.0 copy-start.2
  28.2 1.4 %copy-done.2 = f32[32,18,8,128]{3,2,1,0:T(8,128)} copy-done((f32[32,18,8,128]{3,2,1,0:T(8,128)}, f32[32,18,8,128]{3,2,1,0:T(8,128)S(1)}, u32[]{:S(2)}) %copy-start.2) | copy-done | bytes 2359320
  29.6 0.0 copy-start.11
  29.6 6.0 %all-to-all-start.1 = ((f32[32,18,8,128]{3,2,1,0:T(8,128)}), f32[32,18,8,128]{3,2,1,0:T(8,128)S(1)}, u32[]{:S(2)}, u32[]{:S(2)}) async-start(f32[32,18,8,128]{3,2,1,0:T(8,128)} %copy-done.2), calls=%async_computation.1 | async-start | bytes 4718592 | tf_op jit(solution)/shard_map/all_to_all | solution.py:303
  35.6 0.0 copy-done.10
  35.6 0.0 copy-start.6
  35.6 1.2 copy-done.6
  36.8 0.0 copy-start.8
  36.8 1.6 %copy-done.8 = f32[64,64,128]{2,1,0:T(8,128)S(1)} copy-done((f32[64,64,128]{2,1,0:T(8,128)S(1)}, f32[64,64,128]{2,1,0:T(8,128)}, u32[]{:S(2)}) %copy-start.8) | copy-done | bytes 2097176
  38.4 16.2 %basis.1 = (f32[32,64,128]{2,1,0:T(8,128)}, f32[16,64,128]{2,1,0:T(8,128)}) custom-call(f32[32,64,128]{2,1,0:T(8,128)S(1)} %copy-done.6, f32[16,64,128]{2,1,0:T(8,128)S(1)} %copy-done.10, f32[864,128]{1,0:T(8,128)S(1)} %bitcast.9, f32[64,64,128]{2,1,0:T(8,128)S(1)} %copy-done.8, f32[64,128]{1,0:T(8,128)S(1)} %get-tuple-element.11.rinv_ref), custom_call_target="tpu_custom_call" | custom-call | tf_op jit(solution)/shard_map/basis/pallas_call | solution.py:282
  54.6 0.0 copy-done.11
  54.6 0.0 copy-start.3
  54.6 2.2 %copy-done.3 = f32[64,64,256]{2,1,0:T(8,128)S(1)} copy-done((f32[64,64,256]{2,1,0:T(8,128)S(1)}, f32[64,64,256]{2,1,0:T(8,128)}, u32[]{:S(2)}) %copy-start.3) | copy-done | bytes 4194328
  56.8 0.0 copy-start.4
  56.8 14.4 %left.3.p_ref = bf16[256,64,128]{2,1,0:T(8,128)(2,1)S(1)} custom-call(s32[256]{0:T(256)S(1)} %copy-done.11, f32[864,128]{1,0:T(8,128)S(1)} %bitcast.10, f32[64,64,256]{2,1,0:T(8,128)S(1)} %copy-done.3), custom_call_target="tpu_custom_call" | custom-call | tf_op jit(solution)/shard_map/left/pallas_call | solution.py:159
  71.1 0.0 copy-start.1
  71.1 2.0 %copy-done.1 = bf16[256,64,128]{2,1,0:T(8,128)(2,1)} copy-done((bf16[256,64,128]{2,1,0:T(8,128)(2,1)}, bf16[256,64,128]{2,1,0:T(8,128)(2,1)S(1)}, u32[]{:S(2)}) %copy-start.1) | copy-done | bytes 4194328
  73.2 0.0 copy-done.4
  73.2 0.0 copy-done.12
  73.2 15.2 %left.2.p_ref = bf16[256,64,128]{2,1,0:T(8,128)(2,1)S(1)} custom-call(s32[256]{0:T(256)S(1)} %copy-done.12, f32[864,128]{1,0:T(8,128)S(1)} %bitcast.11, f32[64,64,256]{2,1,0:T(8,128)S(1)} %copy-done.4), custom_call_target="tpu_custom_call" | custom-call | tf_op jit(solution)/shard_map/left/pallas_call | solution.py:159
  88.4 0.0 copy-start
  88.4 1.9 %copy-done = bf16[256,64,128]{2,1,0:T(8,128)(2,1)} copy-done((bf16[256,64,128]{2,1,0:T(8,128)(2,1)}, bf16[256,64,128]{2,1,0:T(8,128)(2,1)S(1)}, u32[]{:S(2)}) %copy-start) | copy-done | bytes 4194328
  90.4 0.0 copy-done.15
  90.4 0.6 fusion
  91.0 0.0 all-to-all-done.1
  91.0 0.0 copy-done.13
  91.0 22.2 %close.3 = f32[64,64,256]{2,1,0:T(8,128)} custom-call(s32[256]{0:T(256)S(1)} %copy-done.13, s32[1]{0:T(128)} %bitcast.5.count_ref, bf16[256,64,128]{2,1,0:T(8,128)(2,1)} %copy-done.1, f32[4608,128]{1,0:T(8,128)S(1)} %bitcast.7), custom_call_target="tpu_custom_call" | custom-call | tf_op jit(solution)/shard_map/close/pallas_call | solution.py:194
  113.1 0.0 copy-done.14
  113.1 22.1 %close.2 = f32[64,64,256]{2,1,0:T(8,128)} custom-call(s32[256]{0:T(256)S(1)} %copy-done.14, s32[1]{0:T(128)} %bitcast.1.count_ref, bf16[256,64,128]{2,1,0:T(8,128)(2,1)} %copy-done, f32[4608,128]{1,0:T(8,128)S(1)} %bitcast.8), custom_call_target="tpu_custom_call" | custom-call | tf_op jit(solution)/shard_map/close/pallas_call | solution.py:194
  (4 shorter events, 0.0 us)
Async XLA Ops:
  4.0 22.5 %all-to-all-start = ((s32[32,1,8]{2,1,0:T(1,128)}), s32[32,1,8]{2,1,0:T(1,128)S(1)}, u32[]{:S(2)}, u32[]{:S(2)}) async-start(s32[32,1,8]{2,1,0:T(1,128)} %bitcast.3), calls=%async_computation | async-start | bytes 32768 | tf_op jit(solution)/shard_map/all_to_all | solution.py:300
  11.3 1.2 copy-start.5
  12.6 1.0 copy-start.9
  13.6 22.0 %copy-start.10 = (f32[16,64,128]{2,1,0:T(8,128)S(1)}, f32[16,64,128]{2,1,0:T(8,128)}, u32[]{:S(2)}) copy-start(f32[16,64,128]{2,1,0:T(8,128)} %e_ref.3) | copy-start | bytes 1572868
  25.2 1.3 copy-start.7
  28.1 1.4 %copy-start.2 = (f32[32,18,8,128]{3,2,1,0:T(8,128)}, f32[32,18,8,128]{3,2,1,0:T(8,128)S(1)}, u32[]{:S(2)}) copy-start(f32[32,18,8,128]{3,2,1,0:T(8,128)S(1)} %gather.1) | copy-start | bytes 7077892
  29.6 25.0 %copy-start.11 = (s32[256]{0:T(256)S(1)}, s32[256]{0:T(256)}, u32[]{:S(2)}) copy-start(s32[256]{0:T(256)} %rows_ref.3) | copy-start | bytes 3076
  29.6 61.4 %all-to-all-start.1 = ((f32[32,18,8,128]{3,2,1,0:T(8,128)}), f32[32,18,8,128]{3,2,1,0:T(8,128)S(1)}, u32[]{:S(2)}, u32[]{:S(2)}) async-start(f32[32,18,8,128]{3,2,1,0:T(8,128)} %copy-done.2), calls=%async_computation.1 | async-start | bytes 4718592 | tf_op jit(solution)/shard_map/all_to_all | solution.py:303
  35.6 1.2 copy-start.6
  36.8 1.6 %copy-start.8 = (f32[64,64,128]{2,1,0:T(8,128)S(1)}, f32[64,64,128]{2,1,0:T(8,128)}, u32[]{:S(2)}) copy-start(f32[64,64,128]{2,1,0:T(8,128)} %copy-done.7) | copy-start | bytes 6291460
  54.6 2.2 %copy-start.3 = (f32[64,64,256]{2,1,0:T(8,128)S(1)}, f32[64,64,256]{2,1,0:T(8,128)}, u32[]{:S(2)}) copy-start(f32[64,64,256]{2,1,0:T(8,128)} %s_ref.3) | copy-start | bytes 12582916
  56.8 16.4 %copy-start.4 = (f32[64,64,256]{2,1,0:T(8,128)S(1)}, f32[64,64,256]{2,1,0:T(8,128)}, u32[]{:S(2)}) copy-start(f32[64,64,256]{2,1,0:T(8,128)} %s_ref.2) | copy-start | bytes 12582916
  56.8 16.4 %copy-start.12 = (s32[256]{0:T(256)S(1)}, s32[256]{0:T(256)}, u32[]{:S(2)}) copy-start(s32[256]{0:T(256)} %rows_ref.2) | copy-start | bytes 3076
  71.1 2.0 %copy-start.1 = (bf16[256,64,128]{2,1,0:T(8,128)(2,1)}, bf16[256,64,128]{2,1,0:T(8,128)(2,1)S(1)}, u32[]{:S(2)}) copy-start(bf16[256,64,128]{2,1,0:T(8,128)(2,1)S(1)} %left.3.p_ref) | copy-start | bytes 12582916
  73.2 17.2 %copy-start.15 = (s32[1,2]{1,0:T(1,128)S(1)}, s32[1,2]{1,0:T(1,128)}, u32[]{:S(2)}) copy-start(s32[1,2]{1,0:T(1,128)} %param.21) | copy-start | bytes 28
  73.2 17.8 %copy-start.13 = (s32[256]{0:T(256)S(1)}, s32[256]{0:T(256)}, u32[]{:S(2)}) copy-start(s32[256]{0:T(256)} %slots_ref.3) | copy-start | bytes 3076
  88.4 1.9 %copy-start = (bf16[256,64,128]{2,1,0:T(8,128)(2,1)}, bf16[256,64,128]{2,1,0:T(8,128)(2,1)S(1)}, u32[]{:S(2)}) copy-start(bf16[256,64,128]{2,1,0:T(8,128)(2,1)S(1)} %left.2.p_ref) | copy-start | bytes 12582916
  91.0 22.2 %copy-start.14 = (s32[256]{0:T(256)S(1)}, s32[256]{0:T(256)}, u32[]{:S(2)}) copy-start(s32[256]{0:T(256)} %slots_ref.2) | copy-start | bytes 3076

commit v2 on v1

v2 whole, which is shorter than its diff:
```python
import functools

import jax
import jax.numpy as jnp
from jax import lax
from jax.experimental import pallas as pl
from jax.experimental.pallas import tpu as pltpu
from jax.sharding import PartitionSpec as P

F32=jnp.float32; BF16=jnp.bfloat16
HI=lax.Precision.HIGHEST
NT=(((1,),(1,)),((),()))
NN=(((1,),(0,)),((),()))

def seg_tiles(k, tiles):
    p, s = divmod(k, 8)
    low = [(8*(tiles-p)+s, jv) for jv in range(tiles-p, tiles)] if p else []
    return low + [(k, jv) for jv in range(p, tiles)]

def chunk_tiles(e):
    if e < 16:
        return seg_tiles(e, 8) + seg_tiles(e+16, 8)
    return [(32 + 4*(e-16) + s, jv) for s in (1, 0, 3, 2) for jv in range(4, 8)]

def params(us, mib):
    return dict(
        cost_estimate=pl.CostEstimate(flops=int(us*1.15e9), bytes_accessed=0, transcendentals=0),
        compiler_params=pltpu.CompilerParams(vmem_limit_bytes=mib*2**20),
    )

def split(x):
    hi = x.astype(BF16)
    return hi, (x - hi.astype(F32)).astype(BF16)

def factor_kernel(u_hbm, e_hbm, table_ref, r_hbm, rinv_ref, nat, gd, a_ref, u_ref, e_ref, r_ref, usem, esem, rsem):
    L = u_ref.shape[0]; Pn = e_ref.shape[0]; C = L+Pn
    part = L//4
    u_in = [pltpu.make_async_copy(u_hbm.at[pl.ds(i*part, part)], u_ref.at[pl.ds(i*part, part)], usem.at[i]) for i in range(4)]
    e_in = pltpu.make_async_copy(e_hbm, e_ref, esem)
    r_out = [pltpu.make_async_copy(r_ref.at[pl.ds(8*p, 8)], r_hbm.at[pl.ds(8*p, 8)], rsem.at[p]) for p in range(8)]
    for copy in u_in + [e_in]:
        copy.start()
    lane = lax.broadcasted_iota(jnp.int32, (64,128), 1)
    left = lane < 64
    left32 = left[:32]
    def gram(l, c):
        u = u_ref[l]
        g = lax.dot_general(u, jnp.concatenate([u,u],0), NT, precision=HI, preferred_element_type=F32)
        gd[l] = g
        nat[pl.ds(l*32,32),:] = jnp.where(left32, g[:32], g[32:])
        return c
    for i in range(4):
        u_in[i].wait()
        lax.fori_loop(i*part, (i+1)*part, gram, 0, unroll=part)
    e_in.wait()
    def parent(p, c):
        e = e_ref[p]
        er = pltpu.roll(e, 64, 1)
        e0 = jnp.where(left, e, er); e1 = jnp.where(left, er, e)
        t0 = lax.dot_general(gd[2*p][:, :64], e0, NN, precision=HI, preferred_element_type=F32)
        t1 = lax.dot_general(gd[2*p+1][:, :64], e1, NN, precision=HI, preferred_element_type=F32)
        est = jnp.concatenate([e0,e1],0).T[:64]
        g = lax.dot_general(est, jnp.concatenate([t0,t1],0), NN, precision=HI, preferred_element_type=F32)
        nat[pl.ds((L+p)*32,32),:] = jnp.where(left32, g[:32], g[32:])
        return c
    lax.fori_loop(0, Pn, parent, 0, unroll=16)
    zeros = jnp.zeros((128-C,128), F32)
    for i in range(32):
        x = jnp.concatenate([nat[pl.ds(i, C, 32), :], zeros], 0).T
        a_ref[i] = x[:64]
        a_ref[i+32] = x[64:]
    live = lax.broadcasted_iota(jnp.int32, (1,128), 1) < C
    sub = lax.broadcasted_iota(jnp.int32, (8,128), 0)
    for p in range(8):
        b = 8*p
        T = [a_ref[b+kk, b:b+8, :] for kk in range(8)]
        for kk in range(8):
            inv = lax.rsqrt(jnp.where(live, T[kk][kk:kk+1,:], 1.0))
            row = jnp.where(sub >= kk, T[kk]*inv, 0.0)
            rinv_ref[pl.ds(b+kk,1), :] = inv
            r_ref[b+kk, b:b+8, :] = row
            for k2 in range(kk+1, 8):
                T[k2] = T[k2] - row[k2:k2+1,:]*row
        for q in range(p+1, 8):
            T = []
            for kk in range(8):
                s = a_ref[b+kk, 8*q:8*q+8, :]
                for t in range(kk):
                    s = s - r_ref[b+t, pl.ds(b+kk,1), :]*T[t]
                T.append(s*rinv_ref[pl.ds(b+kk,1), :])
                r_ref[b+kk, 8*q:8*q+8, :] = T[kk]
        r_out[p].start()
        for q in range(p+1, 8):
            def upd(h, c):
                i0 = 8*q + 4*h
                acc = [[a_ref[i0+u, 8*j:8*j+8, :] for j in range(q,8)] for u in range(4)]
                for kk in range(8):
                    v = [r_ref[b+kk, 8*j:8*j+8, :] for j in range(q,8)]
                    for u in range(4):
                        m = r_ref[b+kk, pl.ds(i0+u,1), :]
                        for j in range(8-q):
                            acc[u][j] = acc[u][j] - m*v[j]
                for u in range(4):
                    for j in range(q,8):
                        a_ref[i0+u, 8*j:8*j+8, :] = acc[u][j-q]
                return c
            lax.fori_loop(0, 2, upd, 0, unroll=True)
    row = lax.broadcasted_iota(jnp.int32, (C,128), 0)
    col = lax.broadcasted_iota(jnp.int32, (C,128), 1)
    eye = (row == col).astype(F32).astype(BF16)
    eye2 = jnp.concatenate([eye, eye], 1)
    for e in range(18):
        ch = jnp.concatenate([r_ref[k, 8*j:8*j+8, :] for k, j in chunk_tiles(e)], 0)
        hi, lo = split(ch)
        table_ref[e] = lax.dot_general(eye2, jnp.concatenate([hi,lo],1), NT, preferred_element_type=F32)
    for copy in r_out:
        copy.wait()

def factor(u, e):
    L, Pn = u.shape[0], e.shape[0]; C = L+Pn
    hbm = pl.BlockSpec(memory_space=pl.ANY)
    vmem = pl.BlockSpec(memory_space=pltpu.VMEM)
    dma = pltpu.SemaphoreType.DMA
    return pl.pallas_call(factor_kernel,
        in_specs=[hbm, hbm], out_specs=(vmem, hbm, vmem),
        out_shape=(jax.ShapeDtypeStruct((18,C,128),F32), jax.ShapeDtypeStruct((64,64,128),F32), jax.ShapeDtypeStruct((64,128),F32)),
        scratch_shapes=[pltpu.VMEM((C*32,128),F32), pltpu.VMEM((L,64,128),F32), pltpu.VMEM((64,64,128),F32),
                        pltpu.VMEM(u.shape,F32), pltpu.VMEM(e.shape,F32), pltpu.VMEM((64,64,128),F32), dma((4,)), dma, dma((8,))],
        **params(11, 60),
        name="factor")(u, e)

def unpack(v):
    lane = lax.broadcasted_iota(jnp.int32, (8,128), 1)
    sub = lax.broadcasted_iota(jnp.int32, (8,128), 0)
    half = lane & 63
    left = lane < 64
    v0, v1 = v[0:8], v[8:16]
    w0, w1 = pltpu.roll(v0, 64, 1), pltpu.roll(v1, 64, 1)
    y = jnp.where(sub < 4, v[16:17], v[17:18])
    z = pltpu.roll(pltpu.roll(y, 0, 1, stride=16, stride_axis=0), 0, 1, stride=16, stride_axis=0)
    parts = [
        jnp.where(left, v0, w0),
        jnp.where(left, v1, w1),
        jnp.where(left, w0, v0),
        jnp.where(left, w1, v1),
        jnp.where(left, z, pltpu.roll(z, 64, 1)),
        jnp.where(left, pltpu.roll(v1, 104, 1), pltpu.roll(v1, 40, 1)),
        jnp.where(left, pltpu.roll(v0, 112, 1), pltpu.roll(v0, 48, 1)),
        jnp.where(left, pltpu.roll(v1, 56, 1), pltpu.roll(v1, 120, 1)),
    ]
    return jnp.concatenate([x if p == 0 else jnp.where(half >= 8*p, x, 0.0) for p, x in enumerate(parts)], 0)

def mix(x):
    left = lax.broadcasted_iota(jnp.int32, x.shape, 1) < 64
    hi = x.astype(BF16).astype(F32)
    return jnp.where(left, hi, x - hi).astype(BF16)

def left_kernel(leaves, lrows_ref, prows_ref, tab_hbm, ls_hbm, ps_hbm, lout_hbm, pout_hbm,
                tab_ref, s_ref, p_ref, m_ref, lhs_ref, tsem, ssem, psem):
    total = lhs_ref.shape[0]
    chunks = s_ref.shape[0]//2
    tab_in = pltpu.make_async_copy(tab_hbm, tab_ref, tsem)
    def s_in(g):
        src, i = (ls_hbm, g) if g < chunks else (ps_hbm, g - chunks)
        return pltpu.make_async_copy(src.at[:, :, pl.ds(i*128, 128)], s_ref.at[g], ssem.at[g])
    def p_out(g):
        dst, i = (lout_hbm, g) if g < chunks else (pout_hbm, g - chunks)
        return pltpu.make_async_copy(p_ref.at[g], dst.at[pl.ds(i*128, 128)], psem.at[g])
    tab_in.start()
    for g in range(2*chunks):
        s_in(g).start()
    tab_in.wait()
    def prep(c, _):
        lhs_ref[c] = mix(unpack(tab_ref[pl.ds(c, 18, total), :]))
        return _
    lax.fori_loop(0, total, prep, 0, unroll=16)
    left = lax.broadcasted_iota(jnp.int32, (32,128), 1) < 64
    def chunk(g, carry):
        for i in range(2*chunks):
            @pl.when(g == i)
            def _():
                s_in(i).wait()
        for k in range(32):
            m_ref[pl.ds(k, 128, 40), :] = jnp.concatenate([s_ref[g, k], s_ref[g, k+32]], 0).T
        low = g < chunks
        start = jnp.where(low, g, g - chunks)*128
        def one(b, _):
            m = m_ref[pl.ds(pl.multiple_of(b*40, 8), 32), :]
            t = pltpu.roll(m, 64, 1)
            hi, lo = split(jnp.concatenate([jnp.where(left, m, t), jnp.where(left, t, m)], 0))
            a = lhs_ref[jnp.where(low, lrows_ref[start + b], leaves + prows_ref[start + b])]
            res = lax.dot_general(jnp.concatenate([a, a], 1), jnp.concatenate([hi,hi,lo,lo], 0), NN, preferred_element_type=F32)
            p_ref[g, b] = mix(res)
            return _
        lax.fori_loop(0, 128, one, 0, unroll=64)
        for i in range(2*chunks):
            @pl.when(g == i)
            def _():
                p_out(i).start()
        return carry
    lax.fori_loop(0, 2*chunks, chunk, 0)
    for g in range(2*chunks):
        p_out(g).wait()

def left_products(lrows, prows, table, lblocks, pblocks, leaves):
    total = table.shape[0]//18
    B = lblocks.shape[2]
    smem = pl.BlockSpec(memory_space=pltpu.SMEM)
    hbm = pl.BlockSpec(memory_space=pl.ANY)
    dma = pltpu.SemaphoreType.DMA
    n = 2*B//128
    return pl.pallas_call(functools.partial(left_kernel, leaves),
        in_specs=[smem, smem, hbm, hbm, hbm], out_specs=(hbm, hbm),
        out_shape=(jax.ShapeDtypeStruct((B,64,128), BF16),)*2,
        scratch_shapes=[pltpu.VMEM(table.shape,F32), pltpu.VMEM((n,64,64,128),F32), pltpu.VMEM((n,128,64,128),BF16),
                        pltpu.VMEM((128*40,128),F32), pltpu.VMEM((total,64,128),BF16), dma, dma((n,)), dma((n,))],
        **params(15, 60), name="left")(lrows, prows, table, lblocks, pblocks)

def close_kernel(caps, hi_ref, lslots_ref, pslots_ref, count_ref, near_hbm, far_hbm, lp_hbm, pp_hbm, lout_hbm, pout_hbm,
                 near_ref, far_ref, p_ref, out_ref, c_ref, w_ref, fsem, psem, osem):
    chunks = p_ref.shape[0]//2
    wide = sum(caps)
    peers = near_ref.shape[0]//(18*wide)
    offset = 2*peers*caps[0]
    near_in = pltpu.make_async_copy(near_hbm, near_ref, fsem.at[0])
    far_in = pltpu.make_async_copy(far_hbm, far_ref, fsem.at[1])
    def p_in(g):
        src, i = (lp_hbm, g) if g < chunks else (pp_hbm, g - chunks)
        return pltpu.make_async_copy(src.at[pl.ds(i*128, 128)], p_ref.at[g], psem.at[g])
    def out(g):
        dst, i = (lout_hbm, g) if g < chunks else (pout_hbm, g - chunks)
        return pltpu.make_async_copy(out_ref.at[g], dst.at[:, :, pl.ds(i*128, 128)], osem.at[g])
    near_in.start()
    far_in.start()
    for g in range(2*chunks):
        p_in(g).start()
    for side, copy, f_ref in ((0, near_in, near_ref), (1, far_in, far_ref)):
        copy.wait()
        first = jnp.where(hi_ref[0] == side, 0, peers)
        def prep(n, _):
            for t in range(wide):
                hi, lo = split(unpack(f_ref[pl.ds(n*18*wide + t, 18, wide), :]))
                spot = (first + n)*caps[0] + t if t < caps[0] else offset + (first + n)*caps[1] + t - caps[0]
                w_ref[spot] = jnp.concatenate([hi, lo], 1)
            return _
        lax.fori_loop(0, peers, prep, 0, unroll=max(1, 16//wide))
    lane = lax.broadcasted_iota(jnp.int32, (64,128), 1)
    def chunk(g, carry):
        for i in range(2*chunks):
            @pl.when(g == i)
            def _():
                p_in(i).wait()
        low = g < chunks
        start = jnp.where(low, g, g - chunks)*128
        def one(b, _):
            a = p_ref[g, b]
            w = w_ref[jnp.where(low, lslots_ref[start + b], offset + pslots_ref[start + b])]
            res = lax.dot_general(jnp.concatenate([a, a], 1), w, NT, preferred_element_type=F32)
            c_ref[pl.ds(pl.multiple_of(b*40, 8), 32), :] = jnp.concatenate([res[:32], res[32:]], 1)
            return _
        lax.fori_loop(0, 128, one, 0, unroll=64)
        live = lane + start < jnp.where(low, count_ref[0, 0], count_ref[0, 1])
        for i in range(32):
            x = c_ref[pl.ds(i, 128, 40), :].T
            out_ref[g, i] = jnp.where(live, x[:64], 0.0)
            out_ref[g, i+32] = jnp.where(live, x[64:], 0.0)
        for i in range(2*chunks):
            @pl.when(g == i)
            def _():
                out(i).start()
        return carry
    lax.fori_loop(0, 2*chunks, chunk, 0)
    for g in range(2*chunks):
        out(g).wait()

def close(hi, lslots, pslots, counts, near, far, lprods, pprods, caps):
    B = lprods.shape[0]
    n = 2*B//128
    total = 2*near.shape[0]//18
    smem = pl.BlockSpec(memory_space=pltpu.SMEM)
    hbm = pl.BlockSpec(memory_space=pl.ANY)
    dma = pltpu.SemaphoreType.DMA
    return pl.pallas_call(functools.partial(close_kernel, caps),
        in_specs=[smem]*4 + [hbm]*4, out_specs=(hbm, hbm),
        out_shape=(jax.ShapeDtypeStruct((64,64,B), F32),)*2,
        scratch_shapes=[pltpu.VMEM(near.shape,F32), pltpu.VMEM(far.shape,F32), pltpu.VMEM((n,128,64,128),BF16),
                        pltpu.VMEM((n,64,64,128),F32), pltpu.VMEM((128*40,128),F32), pltpu.VMEM((total,64,256),BF16),
                        dma((2,)), dma((n,)), dma((n,))],
        **params(19, 60), name="close")(hi, lslots, pslots, counts, near, far, lprods, pprods)

def gather_kernel(picks, lane_ref, idx_ref, table_ref, out_ref):
    peers, wide = idx_ref.shape[0], len(picks)
    C, lanes = table_ref.shape[1], idx_ref.shape[1]
    shape = (peers, wide, lanes)
    pick = lax.broadcasted_iota(jnp.int32, (1, wide, lanes), 1)
    want = jnp.zeros((1, wide, lanes), jnp.int32)
    base = jnp.zeros((1, wide, lanes), jnp.int32)
    for i, (which, t, b) in enumerate(picks):
        want = jnp.where(pick == i, lane_ref[which] + t, want)
        base = jnp.where(pick == i, b, base)
    lane = lax.broadcasted_iota(jnp.int32, shape, 2)
    idx = jnp.where(lane == want, idx_ref[...].reshape(peers, 1, lanes) + base, 0).astype(F32)
    idx = jnp.sum(idx, axis=2, keepdims=True).reshape(peers*wide, 1)
    col = lax.broadcasted_iota(jnp.int32, (peers*wide,128), 1).astype(F32)
    hot = (col == idx).astype(F32).astype(BF16)
    hot = jnp.concatenate([hot, hot], 1)
    pad = jnp.zeros((128-C, 128), F32)
    for e in range(18):
        hi, lo = split(jnp.concatenate([table_ref[e], pad], 0))
        res = lax.dot_general(hot, jnp.concatenate([hi, lo], 0), NN, preferred_element_type=F32)
        for q in range(peers):
            out_ref[pl.ds((q*18 + e)*wide, wide), :] = res[q*wide:(q+1)*wide]

def gather(lanes, idx, table, picks):
    peers, wide = idx.shape[0], len(picks)
    smem = pl.BlockSpec(memory_space=pltpu.SMEM)
    vmem = pl.BlockSpec(memory_space=pltpu.VMEM)
    return pl.pallas_call(functools.partial(gather_kernel, picks),
        in_specs=[smem, vmem, vmem], out_specs=vmem,
        out_shape=jax.ShapeDtypeStruct((peers*18*wide,128),F32),
        **params(2, 60), name="gather")(lanes, idx, table)

def basis_kernel(u_ref, e_ref, table_ref, r_ref, rinv_ref, basis_ref, nt_ref, x_ref, nat):
    L = u_ref.shape[0]; Pn = e_ref.shape[0]; C = L+Pn
    sub = lax.broadcasted_iota(jnp.int32, (8,128), 0)
    zero = jnp.zeros((8,128), F32)
    for q in range(8):
        def rows(h, _):
            acc = [[zero]*q for u in range(4)]
            for t in range(8*q):
                v = [x_ref[t, 8*j:8*j+8, :] for j in range(t//8+1)]
                for u in range(4):
                    m = r_ref[t, pl.ds(8*q+4*h+u,1), :]
                    for j in range(t//8+1):
                        acc[u][j] = acc[u][j] - m*v[j]
            for u in range(4):
                for j in range(q):
                    x_ref[8*q+4*h+u, 8*j:8*j+8, :] = acc[u][j]
            return _
        if q:
            lax.fori_loop(0, 2, rows, 0, unroll=True)
        for j in range(q+1):
            T = []
            for u in range(8):
                s = (sub == u).astype(F32) if j == q else x_ref[8*q+u, 8*j:8*j+8, :]
                for t in range(u):
                    s = s - r_ref[8*q+t, pl.ds(8*q+u,1), :]*T[t]
                T.append(s*rinv_ref[pl.ds(8*q+u,1), :])
                x_ref[8*q+u, 8*j:8*j+8, :] = T[u]
        for j in range(q+1, 8):
            for u in range(8):
                x_ref[8*q+u, 8*j:8*j+8, :] = zero
    for i in range(32):
        nat[pl.ds(i, C, 32), :] = jnp.concatenate([x_ref[i], x_ref[i+32]], 0).T[:C]
    left32 = lax.broadcasted_iota(jnp.int32, (32,128), 1) < 64
    left = lax.broadcasted_iota(jnp.int32, (64,128), 1) < 64
    def twice(m, first, wide):
        t = pltpu.roll(m, 64, 1)
        return jnp.where(wide, m, t) if first else jnp.where(wide, t, m)
    def inverse(c):
        m = nat[pl.ds(c*32,32),:]
        x = mix(jnp.concatenate([twice(m, True, left32), twice(m, False, left32)], 0))
        return jnp.concatenate([x, x], 1)
    def stack(x):
        hi, lo = split(x)
        return jnp.concatenate([hi,hi,lo,lo], 0)
    def leaf(l, _):
        basis_ref[l] = lax.dot_general(inverse(l), stack(u_ref[l]), NN, preferred_element_type=F32)
        return _
    lax.fori_loop(0, L, leaf, 0, unroll=32)
    def parent(p, _):
        e = e_ref[p]
        est = jnp.concatenate([twice(e, True, left), twice(e, False, left)],0).T[:64]
        w = lax.dot_general(inverse(L+p), stack(est), NN, preferred_element_type=F32)
        out = []
        for c in range(2):
            hi, lo = split(twice(w, c == 0, left))
            x = mix(unpack(table_ref[pl.ds(2*p+c, 18, C), :]))
            out.append(lax.dot_general(jnp.concatenate([x,x],1), jnp.concatenate([hi,lo],1), NT, preferred_element_type=F32))
        nt_ref[p] = jnp.concatenate(out, 1)
        return _
    lax.fori_loop(0, Pn, parent, 0, unroll=16)

def bases(u, e, table, r, rinv):
    C = u.shape[0]+e.shape[0]
    return pl.pallas_call(basis_kernel,
        out_shape=(jax.ShapeDtypeStruct(u.shape,F32), jax.ShapeDtypeStruct(e.shape,F32)),
        scratch_shapes=[pltpu.VMEM((64,64,128),F32), pltpu.VMEM((C*32,128),F32)],
        **params(9, 60), name="basis")(u, e, table, r, rinv)

def per_device(
    leaf_bases, transfers, leaf_blocks, parent_blocks, leaf_rows, leaf_slots, leaf_requests,
    parent_rows, parent_slots, parent_requests, block_counts,
):
    leaves = leaf_bases.shape[0]
    parents = transfers.shape[0]
    half = lax.axis_size("lo")
    slots, pslots = leaf_requests.shape[1], parent_requests.shape[1]
    cap, pcap = slots // (2 * half), pslots // (2 * half)
    hi = lax.axis_index("hi").astype(jnp.int32)
    here = hi * half + lax.axis_index("lo").astype(jnp.int32)
    there = (1 - hi) * half + lax.axis_index("lo").astype(jnp.int32)
    lanes = jnp.stack([here * cap, slots + here * pcap, there * cap, slots + there * pcap])
    wanted = jnp.broadcast_to(
        jnp.concatenate([leaf_requests, parent_requests], 1), (half, slots + pslots)
    )
    wanted = lax.all_to_all(wanted, "lo", 0, 0, tiled=True)
    table, r, rinv = factor(leaf_bases, transfers)
    swap = [(0, 1), (1, 0)]
    far_table = lax.ppermute(table, "hi", swap)
    picks = [(0, t, 0) for t in range(cap)] + [(1, t, leaves) for t in range(pcap)]
    near = gather(lanes, wanted, table, picks)
    near = lax.all_to_all(near, "lo", 0, 0, tiled=True)
    flat = table.reshape(-1, 128)
    leaf_left, parent_left = left_products(leaf_rows, parent_rows, flat, leaf_blocks, parent_blocks, leaves)
    far_table, parent_left, leaf_left = lax.optimization_barrier((far_table, parent_left, leaf_left))
    far = gather(lanes, wanted, far_table, [(which + 2, t, base) for which, t, base in picks])
    far = lax.all_to_all(far, "lo", 0, 0, tiled=True)
    leaf_basis, new_transfers = bases(leaf_bases, transfers, flat, r, rinv)
    leaf_coupling, parent_coupling = close(
        hi.reshape(1), leaf_slots, parent_slots, block_counts, near, far, leaf_left, parent_left, (cap, pcap)
    )
    return (leaf_basis, new_transfers, leaf_coupling, parent_coupling)


def solution(mesh):
    halves = jax.sharding.Mesh(mesh.devices.reshape(2, -1), ("hi", "lo"))
    leaf = ("hi", "lo")
    rows = P(leaf, None, None)
    blocks = P(None, None, leaf)
    ids = P(leaf)
    per_owner = P(leaf, None)
    return jax.shard_map(
        per_device,
        mesh=halves,
        in_specs=(rows, rows, blocks, blocks, ids, ids, per_owner, ids, ids, per_owner, per_owner),
        out_specs=(rows, rows, blocks, blocks),
        check_vma=False,
    )
```

time: 136 us -> 102 us (0.75)
  Pallas kernels: 102 us -> 62.3 us
  waiting for transfers between devices: 0.01 us -> 13 us
  local copies, waits for them, and re-layouts: 15.3 us -> 3.04 us
  starting transfers between devices: 13.3 us -> 21.5 us
  other arithmetic: 3.37 us -> 1.26 us
    pallas_call x6 -> x5, Pallas kernels: 86.3 us -> 51.8 us  [the longest x1 19.4 us: close(): pl.pallas_call(functools.partial(close_kernel, caps), in_specs=[smem] * 4...]
    unnamed x33 -> x9, local copies, waits for them, and re-layouts: 14.5 us -> 2.42 us
    all_to_all x2 -> x3, waiting for transfers between devices: 0.01 us -> 7.69 us  [the longest x1 7.25 us: per_device(): far = lax.all_to_all(far, 'lo', 0, 0, tiled=True)]
    pallas_call x1, Pallas kernels: 16.2 us -> 10.5 us  [bases(): pl.pallas_call(basis_kernel, out_shape=(jax.ShapeDtypeStruct(u.shape, F32...]
    all_to_all x2 -> x3, starting transfers between devices: 13.3 us -> 18.9 us  [the longest x1 7.49 us: per_device(): far = lax.all_to_all(far, 'lo', 0, 0, tiled=True)]
    ppermute x0 -> x1, waiting for transfers between devices: none -> 5.32 us  [per_device(): far_table = lax.ppermute(table, 'hi', swap)]
    ppermute x0 -> x1, starting transfers between devices: none -> 2.66 us  [per_device(): far_table = lax.ppermute(table, 'hi', swap)]
  transfers between devices with their start and end apart: 2 -> 4, of which waited for: 0 -> 3; matrix products, arithmetic and copies ran while one was open for 0% -> 1% of each run, Pallas kernels for 42% -> 40%
where the time goes in v2:
time: 102 us
  Pallas kernels  62.3 us (61%)
  starting transfers between devices  21.5 us (21%)
  waiting for transfers between devices  13 us (13%)
  local copies, waits for them, and re-layouts  3.04 us (3%)
  other arithmetic  1.26 us (1%)
    pallas_call x1, Pallas kernels, close(): pl.pallas_call(functools.partial(close_kernel, caps), in_specs=[smem] * 4...  19.4 us
    pallas_call x1, Pallas kernels, left_products(): pl.pallas_call(functools.partial(left_kernel, leaves), in_specs=[smem, sm...  15.3 us
    pallas_call x1, Pallas kernels, factor(): pl.pallas_call(factor_kernel, in_specs=[hbm, hbm], out_specs=(vmem, hbm,...  11.9 us
    pallas_call x1, Pallas kernels, bases(): pl.pallas_call(basis_kernel, out_shape=(jax.ShapeDtypeStruct(u.shape, F32...  10.5 us
    all_to_all x1, starting transfers between devices, per_device(): far = lax.all_to_all(far, 'lo', 0, 0, tiled=True)  7.49 us
    all_to_all x1, waiting for transfers between devices, per_device(): far = lax.all_to_all(far, 'lo', 0, 0, tiled=True)  7.25 us
    all_to_all x1, starting transfers between devices, per_device(): wanted = lax.all_to_all(wanted, 'lo', 0, 0, tiled=True)  6.29 us
    ppermute x1, waiting for transfers between devices, per_device(): far_table = lax.ppermute(table, 'hi', swap)  5.32 us
  transfers between devices with their start and end apart: 4, of which 3 were waited for; matrix products, arithmetic and copies ran while one was open for 1% of the time, Pallas kernels for 40%

profile of v2, /device:TPU:0, one launch (start us, length us, event | category | flops | bytes accessed | tf_op | source)
XLA Modules:
  0.0 102.0 jit_solution(5740852564618096547)
XLA Ops:
  0.6 0.7 pad_add_fusion
  1.3 0.6 broadcast_in_dim.2
  1.9 6.3 %all-to-all-start = ((s32[16,1,256]{2,1,0:T(1,128)}), s32[16,1,256]{2,1,0:T(1,128)S(1)}, u32[]{:S(2)}, u32[]{:S(2)}) async-start(s32[16,1,256]{2,1,0:T(1,128)} %broadcast_in_dim.2), calls=%async_computation | async-start | bytes 32768 | tf_op jit(solution)/shard_map/all_to_all | solution.py:407
  8.2 11.9 %factor.1 = (f32[18,48,128]{2,1,0:T(8,128)}, f32[64,64,128]{2,1,0:T(8,128)}, f32[64,128]{1,0:T(8,128)}) custom-call(f32[32,64,128]{2,1,0:T(8,128)} %u_ref.1, f32[16,64,128]{2,1,0:T(8,128)} %e_ref.1), custom_call_target="tpu_custom_call" | custom-call | flops 12650000384 | tf_op jit(solution)/shard_map/factor/pallas_call | solution.py:124
  20.1 0.6 pad_add_fusion.1.lane_ref
  20.7 0.0 all-to-all-done
  20.7 0.6 copy.17
  21.3 0.0 copy-start.2
  21.3 2.6 %gather.2 = f32[2304,128]{1,0:T(8,128)} custom-call(s32[4]{0:T(128)} %pad_add_fusion.1.lane_ref, s32[16,256]{1,0:T(8,128)} %bitcast.18, f32[18,48,128]{2,1,0:T(8,128)} %get-tuple-element.16.table_ref), custom_call_target="tpu_custom_call" | custom-call | flops 2300000000 | tf_op jit(solution)/shard_map/gather/pallas_call | solution.py:318
  24.0 5.1 %all-to-all-start.1 = ((f32[16,144,128]{2,1,0:T(8,128)}), f32[16,144,128]{2,1,0:T(8,128)S(1)}, u32[]{:S(2)}, u32[]{:S(2)}) async-start(f32[16,144,128]{2,1,0:T(8,128)} %bitcast.16), calls=%async_computation.1 | async-start | bytes 2359296 | tf_op jit(solution)/shard_map/all_to_all | solution.py:413
  29.1 0.0 copy-done.2
  29.1 2.7 %collective-permute-start = (f32[18,48,128]{2,1,0:T(8,128)S(1)}, f32[18,48,128]{2,1,0:T(8,128)S(1)}, u32[]{:S(2)}, u32[]{:S(2)}) collective-permute-start(f32[18,48,128]{2,1,0:T(8,128)S(1)} %copy-done.2), channel_id=1, source_target_pairs={{0,16},{16,0},{1,17},{17,1},{2,18},{18,2},{3,19},{19,3},{4,20},{20... | collective-permute-start | bytes 1327112 | tf_op jit(solution)/shard_map/ppermute | solution.py:410
  31.7 15.3 %left.1 = (bf16[256,64,128]{2,1,0:T(8,128)(2,1)}, bf16[256,64,128]{2,1,0:T(8,128)(2,1)}) custom-call(s32[256]{0:T(256)} %lrows_ref.1, s32[256]{0:T(256)} %prows_ref.1, f32[864,128]{1,0:T(8,128)} %bitcast.21, f32[64,64,256]{2,1,0:T(8,128)} %ls_hbm.1, f32[64,64,256]{2,1,0:T(8,128)} %ps_hbm.1), custom_call_target="tpu_custom_call" | custom-call | flops 17250000896 | tf_op jit(solution)/shard_map/left/pallas_call | solution.py:212
  47.0 5.3 %collective-permute-done.table_ref = f32[18,48,128]{2,1,0:T(8,128)S(1)} collective-permute-done((f32[18,48,128]{2,1,0:T(8,128)S(1)}, f32[18,48,128]{2,1,0:T(8,128)S(1)}, u32[]{:S(2)}, u32[]{:S(2)}) %collective-permute-start) | collective-permute-done | bytes 442400 | tf_op jit(solution)/shard_map/ppermute | solution.py:410
  52.4 0.0 copy-start.3
  52.4 0.8 copy-done.3
  53.1 2.6 %gather.3 = f32[2304,128]{1,0:T(8,128)} custom-call(s32[4]{0:T(128)} %pad_add_fusion.1.lane_ref, s32[16,256]{1,0:T(8,128)} %bitcast.19, f32[18,48,128]{2,1,0:T(8,128)} %copy-done.3), custom_call_target="tpu_custom_call" | custom-call | flops 2300000000 | tf_op jit(solution)/shard_map/gather/pallas_call | solution.py:318
  55.7 0.4 all-to-all-done.1
  56.2 0.0 copy-start
  56.2 7.5 %all-to-all-start.2 = ((f32[16,144,128]{2,1,0:T(8,128)}), f32[16,144,128]{2,1,0:T(8,128)S(1)}, u32[]{:S(2)}, u32[]{:S(2)}) async-start(f32[16,144,128]{2,1,0:T(8,128)} %bitcast.17), calls=%async_computation.2 | async-start | bytes 2359296 | tf_op jit(solution)/shard_map/all_to_all | solution.py:418
  63.7 10.5 %basis.1 = (f32[32,64,128]{2,1,0:T(8,128)}, f32[16,64,128]{2,1,0:T(8,128)}) custom-call(f32[32,64,128]{2,1,0:T(8,128)} %u_ref.1, f32[16,64,128]{2,1,0:T(8,128)} %e_ref.1, f32[864,128]{1,0:T(8,128)} %bitcast.22, f32[64,64,128]{2,1,0:T(8,128)} %get-tuple-element.17.r_ref, f32[64,128]{1,0:T(8,128)} %get-tuple-element.18.rinv_ref), custom_call_target="tpu_custom_call" | custom-call | flops 10350000128 | tf_op jit(solution)/shard_map/basis/pallas_call | solution.py:386
  74.2 0.0 copy-done
  74.2 7.3 %all-to-all-done.2 = f32[16,144,128]{2,1,0:T(8,128)S(1)} async-done(((f32[16,144,128]{2,1,0:T(8,128)}), f32[16,144,128]{2,1,0:T(8,128)S(1)}, u32[]{:S(2)}, u32[]{:S(2)}) %all-to-all-start.2) | async-done | bytes 1179680 | tf_op jit(solution)/shard_map/all_to_all | solution.py:418
  81.4 0.0 copy-start.1
  81.4 1.0 %copy-done.1 = f32[16,144,128]{2,1,0:T(8,128)} copy-done((f32[16,144,128]{2,1,0:T(8,128)}, f32[16,144,128]{2,1,0:T(8,128)S(1)}, u32[]{:S(2)}) %copy-start.1) | copy-done | bytes 1179672
  82.5 19.4 %close.1 = (f32[64,64,256]{2,1,0:T(8,128)}, f32[64,64,256]{2,1,0:T(8,128)}) custom-call(s32[1]{0:T(128)} %bitcast.1.hi_ref, s32[256]{0:T(256)} %lslots_ref.1, s32[256]{0:T(256)} %pslots_ref.1, s32[1,2]{1,0:T(1,128)} %count_ref.1, f32[2304,128]{1,0:T(8,128)} %bitcast.14, f32[2304,128]{1,0:T(8,128)} %bitcast.15, ...), custom_call_target="tpu_custom_call" | custom-call | flops 21849999360 | tf_op jit(solution)/shard_map/close/pallas_call | solution.py:283
Async XLA Ops:
  1.9 18.8 %all-to-all-start = ((s32[16,1,256]{2,1,0:T(1,128)}), s32[16,1,256]{2,1,0:T(1,128)S(1)}, u32[]{:S(2)}, u32[]{:S(2)}) async-start(s32[16,1,256]{2,1,0:T(1,128)} %broadcast_in_dim.2), calls=%async_computation | async-start | bytes 32768 | tf_op jit(solution)/shard_map/all_to_all | solution.py:407
  21.3 7.7 %copy-start.2 = (f32[18,48,128]{2,1,0:T(8,128)S(1)}, f32[18,48,128]{2,1,0:T(8,128)}, u32[]{:S(2)}) copy-start(f32[18,48,128]{2,1,0:T(8,128)} %get-tuple-element.16.table_ref) | copy-start | bytes 1327108
  24.0 32.2 %all-to-all-start.1 = ((f32[16,144,128]{2,1,0:T(8,128)}), f32[16,144,128]{2,1,0:T(8,128)S(1)}, u32[]{:S(2)}, u32[]{:S(2)}) async-start(f32[16,144,128]{2,1,0:T(8,128)} %bitcast.16), calls=%async_computation.1 | async-start | bytes 2359296 | tf_op jit(solution)/shard_map/all_to_all | solution.py:413
  29.1 23.3 %collective-permute-start = (f32[18,48,128]{2,1,0:T(8,128)S(1)}, f32[18,48,128]{2,1,0:T(8,128)S(1)}, u32[]{:S(2)}, u32[]{:S(2)}) collective-permute-start(f32[18,48,128]{2,1,0:T(8,128)S(1)} %copy-done.2), channel_id=1, source_target_pairs={{0,16},{16,0},{1,17},{17,1},{2,18},{18,2},{3,19},{19,3},{4,20},{20... | collective-permute-start | bytes 1327112 | tf_op jit(solution)/shard_map/ppermute | solution.py:410
  52.4 0.8 copy-start.3
  56.2 18.0 %copy-start = (f32[16,144,128]{2,1,0:T(8,128)}, f32[16,144,128]{2,1,0:T(8,128)S(1)}, u32[]{:S(2)}) copy-start(f32[16,144,128]{2,1,0:T(8,128)S(1)} %all-to-all-done.1) | copy-start | bytes 3538948
  56.2 25.3 %all-to-all-start.2 = ((f32[16,144,128]{2,1,0:T(8,128)}), f32[16,144,128]{2,1,0:T(8,128)S(1)}, u32[]{:S(2)}, u32[]{:S(2)}) async-start(f32[16,144,128]{2,1,0:T(8,128)} %bitcast.17), calls=%async_computation.2 | async-start | bytes 2359296 | tf_op jit(solution)/shard_map/all_to_all | solution.py:418
  81.4 1.0 %copy-start.1 = (f32[16,144,128]{2,1,0:T(8,128)}, f32[16,144,128]{2,1,0:T(8,128)S(1)}, u32[]{:S(2)}) copy-start(f32[16,144,128]{2,1,0:T(8,128)S(1)} %all-to-all-done.2) | copy-start | bytes 3538948

commit v3 on v2

--- a/solution.py
+++ b/solution.py
@@ -47,7 +47,7 @@
         u = u_ref[l]
         g = lax.dot_general(u, jnp.concatenate([u,u],0), NT, precision=HI, preferred_element_type=F32)
         gd[l] = g
-        nat[pl.ds(l*32,32),:] = jnp.where(left32, g[:32], g[32:])
+        nat[pl.ds(l*40,32),:] = jnp.where(left32, g[:32], g[32:])
         return c
     for i in range(4):
         u_in[i].wait()
@@ -61,12 +61,12 @@
         t1 = lax.dot_general(gd[2*p+1][:, :64], e1, NN, precision=HI, preferred_element_type=F32)
         est = jnp.concatenate([e0,e1],0).T[:64]
         g = lax.dot_general(est, jnp.concatenate([t0,t1],0), NN, precision=HI, preferred_element_type=F32)
-        nat[pl.ds((L+p)*32,32),:] = jnp.where(left32, g[:32], g[32:])
+        nat[pl.ds((L+p)*40,32),:] = jnp.where(left32, g[:32], g[32:])
         return c
     lax.fori_loop(0, Pn, parent, 0, unroll=16)
     zeros = jnp.zeros((128-C,128), F32)
     for i in range(32):
-        x = jnp.concatenate([nat[pl.ds(i, C, 32), :], zeros], 0).T
+        x = jnp.concatenate([nat[pl.ds(i, C, 40), :], zeros], 0).T
         a_ref[i] = x[:64]
         a_ref[i+32] = x[64:]
     live = lax.broadcasted_iota(jnp.int32, (1,128), 1) < C
@@ -124,7 +124,7 @@
     return pl.pallas_call(factor_kernel,
         in_specs=[hbm, hbm], out_specs=(vmem, hbm, vmem),
         out_shape=(jax.ShapeDtypeStruct((18,C,128),F32), jax.ShapeDtypeStruct((64,64,128),F32), jax.ShapeDtypeStruct((64,128),F32)),
-        scratch_shapes=[pltpu.VMEM((C*32,128),F32), pltpu.VMEM((L,64,128),F32), pltpu.VMEM((64,64,128),F32),
+        scratch_shapes=[pltpu.VMEM((C*40,128),F32), pltpu.VMEM((L,64,128),F32), pltpu.VMEM((64,64,128),F32),
                         pltpu.VMEM(u.shape,F32), pltpu.VMEM(e.shape,F32), pltpu.VMEM((64,64,128),F32), dma((4,)), dma, dma((8,))],
         **params(11, 60),
         name="factor")(u, e)
@@ -155,95 +155,105 @@
     hi = x.astype(BF16).astype(F32)
     return jnp.where(left, hi, x - hi).astype(BF16)
 
-def left_kernel(leaves, lrows_ref, prows_ref, tab_hbm, ls_hbm, ps_hbm, lout_hbm, pout_hbm,
-                tab_ref, s_ref, p_ref, m_ref, lhs_ref, tsem, ssem, psem):
-    total = lhs_ref.shape[0]
-    chunks = s_ref.shape[0]//2
-    tab_in = pltpu.make_async_copy(tab_hbm, tab_ref, tsem)
-    def s_in(g):
-        src, i = (ls_hbm, g) if g < chunks else (ps_hbm, g - chunks)
-        return pltpu.make_async_copy(src.at[:, :, pl.ds(i*128, 128)], s_ref.at[g], ssem.at[g])
-    def p_out(g):
-        dst, i = (lout_hbm, g) if g < chunks else (pout_hbm, g - chunks)
-        return pltpu.make_async_copy(p_ref.at[g], dst.at[pl.ds(i*128, 128)], psem.at[g])
-    tab_in.start()
-    for g in range(2*chunks):
-        s_in(g).start()
-    tab_in.wait()
+LEFT_US = 40
+
+def left_kernel(base, total, rows_ref, tab_ref, s_hbm, out_hbm, s_ref, p_ref, m_ref, lhs_ref, ssem, psem):
+    chunks = s_ref.shape[0]
+    s_in = [pltpu.make_async_copy(s_hbm.at[:, :, pl.ds(g*128, 128)], s_ref.at[g], ssem.at[g]) for g in range(chunks)]
+    p_out = [pltpu.make_async_copy(p_ref.at[g], out_hbm.at[pl.ds(g*128, 128)], psem.at[g]) for g in range(chunks)]
+    for copy in s_in:
+        copy.start()
     def prep(c, _):
-        lhs_ref[c] = mix(unpack(tab_ref[pl.ds(c, 18, total), :]))
+        lhs_ref[c] = mix(unpack(tab_ref[pl.ds(base + c, 18, total), :]))
         return _
-    lax.fori_loop(0, total, prep, 0, unroll=16)
+    lax.fori_loop(0, lhs_ref.shape[0], prep, 0, unroll=16)
     left = lax.broadcasted_iota(jnp.int32, (32,128), 1) < 64
-    def chunk(g, carry):
-        for i in range(2*chunks):
-            @pl.when(g == i)
-            def _():
-                s_in(i).wait()
+    for g in range(chunks):
+        s_in[g].wait()
         for k in range(32):
             m_ref[pl.ds(k, 128, 40), :] = jnp.concatenate([s_ref[g, k], s_ref[g, k+32]], 0).T
-        low = g < chunks
-        start = jnp.where(low, g, g - chunks)*128
         def one(b, _):
             m = m_ref[pl.ds(pl.multiple_of(b*40, 8), 32), :]
             t = pltpu.roll(m, 64, 1)
             hi, lo = split(jnp.concatenate([jnp.where(left, m, t), jnp.where(left, t, m)], 0))
-            a = lhs_ref[jnp.where(low, lrows_ref[start + b], leaves + prows_ref[start + b])]
+            a = lhs_ref[rows_ref[g*128 + b]]
             res = lax.dot_general(jnp.concatenate([a, a], 1), jnp.concatenate([hi,hi,lo,lo], 0), NN, preferred_element_type=F32)
             p_ref[g, b] = mix(res)
             return _
         lax.fori_loop(0, 128, one, 0, unroll=64)
-        for i in range(2*chunks):
-            @pl.when(g == i)
-            def _():
-                p_out(i).start()
-        return carry
-    lax.fori_loop(0, 2*chunks, chunk, 0)
-    for g in range(2*chunks):
-        p_out(g).wait()
-
-def left_products(lrows, prows, table, lblocks, pblocks, leaves):
+        p_out[g].start()
+    for copy in p_out:
+        copy.wait()
+
+def left_products(rows, table, blocks, base, clusters):
     total = table.shape[0]//18
-    B = lblocks.shape[2]
-    smem = pl.BlockSpec(memory_space=pltpu.SMEM)
+    B = blocks.shape[2]
+    n = B//128
     hbm = pl.BlockSpec(memory_space=pl.ANY)
     dma = pltpu.SemaphoreType.DMA
-    n = 2*B//128
-    return pl.pallas_call(functools.partial(left_kernel, leaves),
-        in_specs=[smem, smem, hbm, hbm, hbm], out_specs=(hbm, hbm),
-        out_shape=(jax.ShapeDtypeStruct((B,64,128), BF16),)*2,
-        scratch_shapes=[pltpu.VMEM(table.shape,F32), pltpu.VMEM((n,64,64,128),F32), pltpu.VMEM((n,128,64,128),BF16),
-                        pltpu.VMEM((128*40,128),F32), pltpu.VMEM((total,64,128),BF16), dma, dma((n,)), dma((n,))],
-        **params(15, 60), name="left")(lrows, prows, table, lblocks, pblocks)
-
-def close_kernel(caps, hi_ref, lslots_ref, pslots_ref, count_ref, near_hbm, far_hbm, lp_hbm, pp_hbm, lout_hbm, pout_hbm,
-                 near_ref, far_ref, p_ref, out_ref, c_ref, w_ref, fsem, psem, osem):
+    return pl.pallas_call(functools.partial(left_kernel, base, total),
+        in_specs=[pl.BlockSpec(memory_space=pltpu.SMEM), pl.BlockSpec(memory_space=pltpu.VMEM), hbm], out_specs=hbm,
+        out_shape=jax.ShapeDtypeStruct((B,64,128), BF16),
+        scratch_shapes=[pltpu.VMEM((n,64,64,128),F32), pltpu.VMEM((n,128,64,128),BF16),
+                        pltpu.VMEM((128*40,128),F32), pltpu.VMEM((clusters,64,128),BF16), dma((n,)), dma((n,))],
+        **params(LEFT_US, 60), name="left")(rows, table, blocks)
+
+def weights(f_ref, first, stride):
+    hi, lo = split(unpack(f_ref[pl.ds(first, 18, stride), :]))
+    return jnp.concatenate([hi, lo], 1)
+
+def unpack_kernel(caps, near_ref, w_hbm, w_ref, sem):
+    wide = sum(caps)
+    peers = near_ref.shape[0]//(18*wide)
+    def prep(n, _):
+        for t in range(wide):
+            spot = n*caps[0] + t if t < caps[0] else peers*caps[0] + n*caps[1] + t - caps[0]
+            w_ref[spot] = weights(near_ref, n*18*wide + t, wide)
+        return _
+    lax.fori_loop(0, peers, prep, 0, unroll=max(1, 16//wide))
+    copy = pltpu.make_async_copy(w_ref, w_hbm, sem)
+    copy.start()
+    copy.wait()
+
+def unpack_near(near, caps):
+    total = near.shape[0]//18
+    return pl.pallas_call(functools.partial(unpack_kernel, caps),
+        in_specs=[pl.BlockSpec(memory_space=pltpu.VMEM)], out_specs=pl.BlockSpec(memory_space=pl.ANY),
+        out_shape=jax.ShapeDtypeStruct((total,64,256), BF16),
+        scratch_shapes=[pltpu.VMEM((total,64,256), BF16), pltpu.SemaphoreType.DMA],
+        **params(5, 60), name="unpack")(near)
+
+def close_kernel(caps, lslots_ref, pslots_ref, count_ref, near_hbm, far_ref, lp_hbm, pp_hbm, lout_hbm, pout_hbm,
+                 p_ref, out_ref, c_ref, w_ref, wsem, psem, osem):
     chunks = p_ref.shape[0]//2
     wide = sum(caps)
-    peers = near_ref.shape[0]//(18*wide)
+    peers = far_ref.shape[0]//(18*wide)
     offset = 2*peers*caps[0]
-    near_in = pltpu.make_async_copy(near_hbm, near_ref, fsem.at[0])
-    far_in = pltpu.make_async_copy(far_hbm, far_ref, fsem.at[1])
+    hi = lax.axis_index("hi")
+    sizes = (peers*caps[0], peers*caps[1])
+    w_in = [pltpu.make_async_copy(near_hbm.at[pl.ds(i*sizes[0], sizes[i])], w_ref.at[pl.ds(i*offset + hi*sizes[i], sizes[i])], wsem.at[i])
+            for i in range(2)]
     def p_in(g):
         src, i = (lp_hbm, g) if g < chunks else (pp_hbm, g - chunks)
         return pltpu.make_async_copy(src.at[pl.ds(i*128, 128)], p_ref.at[g], psem.at[g])
     def out(g):
         dst, i = (lout_hbm, g) if g < chunks else (pout_hbm, g - chunks)
         return pltpu.make_async_copy(out_ref.at[g], dst.at[:, :, pl.ds(i*128, 128)], osem.at[g])
-    near_in.start()
-    far_in.start()
-    for g in range(2*chunks):
+    for g in range(chunks):
         p_in(g).start()
-    for side, copy, f_ref in ((0, near_in, near_ref), (1, far_in, far_ref)):
+    for copy in w_in:
+        copy.start()
+    for g in range(chunks, 2*chunks):
+        p_in(g).start()
+    def prep(n, _):
+        device = (1 - hi)*peers + n
+        for t in range(wide):
+            spot = device*caps[0] + t if t < caps[0] else offset + device*caps[1] + t - caps[0]
+            w_ref[spot] = weights(far_ref, n*18*wide + t, wide)
+        return _
+    lax.fori_loop(0, peers, prep, 0, unroll=max(1, 16//wide))
+    for copy in w_in:
         copy.wait()
-        first = jnp.where(hi_ref[0] == side, 0, peers)
-        def prep(n, _):
-            for t in range(wide):
-                hi, lo = split(unpack(f_ref[pl.ds(n*18*wide + t, 18, wide), :]))
-                spot = (first + n)*caps[0] + t if t < caps[0] else offset + (first + n)*caps[1] + t - caps[0]
-                w_ref[spot] = jnp.concatenate([hi, lo], 1)
-            return _
-        lax.fori_loop(0, peers, prep, 0, unroll=max(1, 16//wide))
     lane = lax.broadcasted_iota(jnp.int32, (64,128), 1)
     def chunk(g, carry):
         for i in range(2*chunks):
@@ -273,30 +283,35 @@
     for g in range(2*chunks):
         out(g).wait()
 
-def close(hi, lslots, pslots, counts, near, far, lprods, pprods, caps):
+def close(lslots, pslots, counts, near, far, lprods, pprods, caps):
     B = lprods.shape[0]
     n = 2*B//128
-    total = 2*near.shape[0]//18
+    total = 2*near.shape[0]
     smem = pl.BlockSpec(memory_space=pltpu.SMEM)
     hbm = pl.BlockSpec(memory_space=pl.ANY)
     dma = pltpu.SemaphoreType.DMA
     return pl.pallas_call(functools.partial(close_kernel, caps),
-        in_specs=[smem]*4 + [hbm]*4, out_specs=(hbm, hbm),
+        in_specs=[smem]*3 + [hbm, pl.BlockSpec(memory_space=pltpu.VMEM)] + [hbm]*2, out_specs=(hbm, hbm),
         out_shape=(jax.ShapeDtypeStruct((64,64,B), F32),)*2,
-        scratch_shapes=[pltpu.VMEM(near.shape,F32), pltpu.VMEM(far.shape,F32), pltpu.VMEM((n,128,64,128),BF16),
+        scratch_shapes=[pltpu.VMEM((n,128,64,128),BF16),
                         pltpu.VMEM((n,64,64,128),F32), pltpu.VMEM((128*40,128),F32), pltpu.VMEM((total,64,256),BF16),
                         dma((2,)), dma((n,)), dma((n,))],
-        **params(19, 60), name="close")(hi, lslots, pslots, counts, near, far, lprods, pprods)
-
-def gather_kernel(picks, lane_ref, idx_ref, table_ref, out_ref):
+        **params(19, 60), name="close")(lslots, pslots, counts, near, far, lprods, pprods)
+
+def gather_kernel(picks, sizes, far, idx_ref, table_ref, out_ref):
     peers, wide = idx_ref.shape[0], len(picks)
     C, lanes = table_ref.shape[1], idx_ref.shape[1]
     shape = (peers, wide, lanes)
+    half, slots, cap, pcap = sizes
+    hi = lax.axis_index("hi")
+    side = 1 - hi if far else hi
+    place = side*half + lax.axis_index("lo")
+    starts = (place*cap, slots + place*pcap)
     pick = lax.broadcasted_iota(jnp.int32, (1, wide, lanes), 1)
     want = jnp.zeros((1, wide, lanes), jnp.int32)
     base = jnp.zeros((1, wide, lanes), jnp.int32)
     for i, (which, t, b) in enumerate(picks):
-        want = jnp.where(pick == i, lane_ref[which] + t, want)
+        want = jnp.where(pick == i, starts[which] + t, want)
         base = jnp.where(pick == i, b, base)
     lane = lax.broadcasted_iota(jnp.int32, shape, 2)
     idx = jnp.where(lane == want, idx_ref[...].reshape(peers, 1, lanes) + base, 0).astype(F32)
@@ -311,20 +326,27 @@
         for q in range(peers):
             out_ref[pl.ds((q*18 + e)*wide, wide), :] = res[q*wide:(q+1)*wide]
 
-def gather(lanes, idx, table, picks):
+def gather(idx, table, picks, sizes, far):
     peers, wide = idx.shape[0], len(picks)
-    smem = pl.BlockSpec(memory_space=pltpu.SMEM)
     vmem = pl.BlockSpec(memory_space=pltpu.VMEM)
-    return pl.pallas_call(functools.partial(gather_kernel, picks),
-        in_specs=[smem, vmem, vmem], out_specs=vmem,
+    return pl.pallas_call(functools.partial(gather_kernel, picks, sizes, far),
+        in_specs=[vmem, vmem], out_specs=vmem,
         out_shape=jax.ShapeDtypeStruct((peers*18*wide,128),F32),
-        **params(2, 60), name="gather")(lanes, idx, table)
-
-def basis_kernel(u_ref, e_ref, table_ref, r_ref, rinv_ref, basis_ref, nt_ref, x_ref, nat):
+        **params(0.1, 60), name="gather")(idx, table)
+
+def basis_kernel(u_hbm, e_hbm, table_ref, r_hbm, rinv_ref, basis_hbm, nt_hbm, x_ref, nat, u_ref, e_ref, r_ref, basis_ref, nt_ref, rsem, sem):
     L = u_ref.shape[0]; Pn = e_ref.shape[0]; C = L+Pn
+    r_in = [pltpu.make_async_copy(r_hbm.at[pl.ds(8*p, 8)], r_ref.at[pl.ds(8*p, 8)], rsem.at[p]) for p in range(8)]
+    u_in = pltpu.make_async_copy(u_hbm, u_ref, sem.at[0])
+    e_in = pltpu.make_async_copy(e_hbm, e_ref, sem.at[1])
+    basis_out = pltpu.make_async_copy(basis_ref, basis_hbm, sem.at[2])
+    nt_out = pltpu.make_async_copy(nt_ref, nt_hbm, sem.at[3])
+    for copy in r_in + [u_in, e_in]:
+        copy.start()
     sub = lax.broadcasted_iota(jnp.int32, (8,128), 0)
     zero = jnp.zeros((8,128), F32)
     for q in range(8):
+        r_in[q].wait()
         def rows(h, _):
             acc = [[zero]*q for u in range(4)]
             for t in range(8*q):
@@ -351,14 +373,14 @@
             for u in range(8):
                 x_ref[8*q+u, 8*j:8*j+8, :] = zero
     for i in range(32):
-        nat[pl.ds(i, C, 32), :] = jnp.concatenate([x_ref[i], x_ref[i+32]], 0).T[:C]
+        nat[pl.ds(i, C, 40), :] = jnp.concatenate([x_ref[i], x_ref[i+32]], 0).T[:C]
     left32 = lax.broadcasted_iota(jnp.int32, (32,128), 1) < 64
     left = lax.broadcasted_iota(jnp.int32, (64,128), 1) < 64
     def twice(m, first, wide):
         t = pltpu.roll(m, 64, 1)
         return jnp.where(wide, m, t) if first else jnp.where(wide, t, m)
     def inverse(c):
-        m = nat[pl.ds(c*32,32),:]
+        m = nat[pl.ds(c*40,32),:]
         x = mix(jnp.concatenate([twice(m, True, left32), twice(m, False, left32)], 0))
         return jnp.concatenate([x, x], 1)
     def stack(x):
@@ -367,7 +389,10 @@
     def leaf(l, _):
         basis_ref[l] = lax.dot_general(inverse(l), stack(u_ref[l]), NN, preferred_element_type=F32)
         return _
+    u_in.wait()
     lax.fori_loop(0, L, leaf, 0, unroll=32)
+    basis_out.start()
+    e_in.wait()
     def parent(p, _):
         e = e_ref[p]
         est = jnp.concatenate([twice(e, True, left), twice(e, False, left)],0).T[:64]
@@ -380,12 +405,20 @@
         nt_ref[p] = jnp.concatenate(out, 1)
         return _
     lax.fori_loop(0, Pn, parent, 0, unroll=16)
+    nt_out.start()
+    basis_out.wait()
+    nt_out.wait()
 
 def bases(u, e, table, r, rinv):
     C = u.shape[0]+e.shape[0]
+    hbm = pl.BlockSpec(memory_space=pl.ANY)
+    vmem = pl.BlockSpec(memory_space=pltpu.VMEM)
+    dma = pltpu.SemaphoreType.DMA
     return pl.pallas_call(basis_kernel,
+        in_specs=[hbm, hbm, vmem, hbm, vmem], out_specs=(hbm, hbm),
         out_shape=(jax.ShapeDtypeStruct(u.shape,F32), jax.ShapeDtypeStruct(e.shape,F32)),
-        scratch_shapes=[pltpu.VMEM((64,64,128),F32), pltpu.VMEM((C*32,128),F32)],
+        scratch_shapes=[pltpu.VMEM((64,64,128),F32), pltpu.VMEM((C*40,128),F32), pltpu.VMEM(u.shape,F32), pltpu.VMEM(e.shape,F32),
+                        pltpu.VMEM((64,64,128),F32), pltpu.VMEM(u.shape,F32), pltpu.VMEM(e.shape,F32), dma((8,)), dma((4,))],
         **params(9, 60), name="basis")(u, e, table, r, rinv)
 
 def per_device(
@@ -397,28 +430,27 @@
     half = lax.axis_size("lo")
     slots, pslots = leaf_requests.shape[1], parent_requests.shape[1]
     cap, pcap = slots // (2 * half), pslots // (2 * half)
-    hi = lax.axis_index("hi").astype(jnp.int32)
-    here = hi * half + lax.axis_index("lo").astype(jnp.int32)
-    there = (1 - hi) * half + lax.axis_index("lo").astype(jnp.int32)
-    lanes = jnp.stack([here * cap, slots + here * pcap, there * cap, slots + there * pcap])
-    wanted = jnp.broadcast_to(
-        jnp.concatenate([leaf_requests, parent_requests], 1), (half, slots + pslots)
+    wanted = jnp.concatenate(
+        [jnp.broadcast_to(x, (half, x.shape[1])) for x in (leaf_requests, parent_requests)], 1
     )
     wanted = lax.all_to_all(wanted, "lo", 0, 0, tiled=True)
     table, r, rinv = factor(leaf_bases, transfers)
-    swap = [(0, 1), (1, 0)]
-    far_table = lax.ppermute(table, "hi", swap)
+    far_table = lax.ppermute(table, "hi", [(0, 1), (1, 0)])
     picks = [(0, t, 0) for t in range(cap)] + [(1, t, leaves) for t in range(pcap)]
-    near = gather(lanes, wanted, table, picks)
+    sizes = (half, slots, cap, pcap)
+    near = gather(wanted, table, picks, sizes, False)
+    flat = lax.optimization_barrier((table, near))[0].reshape(-1, 128)
     near = lax.all_to_all(near, "lo", 0, 0, tiled=True)
-    flat = table.reshape(-1, 128)
-    leaf_left, parent_left = left_products(leaf_rows, parent_rows, flat, leaf_blocks, parent_blocks, leaves)
-    far_table, parent_left, leaf_left = lax.optimization_barrier((far_table, parent_left, leaf_left))
-    far = gather(lanes, wanted, far_table, [(which + 2, t, base) for which, t, base in picks])
+    leaf_left = left_products(leaf_rows, flat, leaf_blocks, 0, leaves)
+    parent_left = left_products(parent_rows, flat, parent_blocks, leaves, parents)
+    far_table = lax.optimization_barrier((far_table, leaf_left, parent_left))[0]
+    far = gather(wanted, far_table, picks, sizes, True)
+    r = lax.optimization_barrier((r, far))[0]
+    near = unpack_near(lax.optimization_barrier((near, far))[0], (cap, pcap))
     far = lax.all_to_all(far, "lo", 0, 0, tiled=True)
     leaf_basis, new_transfers = bases(leaf_bases, transfers, flat, r, rinv)
     leaf_coupling, parent_coupling = close(
-        hi.reshape(1), leaf_slots, parent_slots, block_counts, near, far, leaf_left, parent_left, (cap, pcap)
+        leaf_slots, parent_slots, block_counts, near, far, leaf_left, parent_left, (cap, pcap)
     )
     return (leaf_basis, new_transfers, leaf_coupling, parent_coupling)
 

time: 102 us -> 96.1 us (0.942)
  waiting for transfers between devices: 13 us -> 6.17 us
  Pallas kernels: 62.3 us -> 66.8 us
  starting transfers between devices: 21.5 us -> 18 us
    all_to_all x1, waiting for transfers between devices: 7.25 us -> 0.64 us  [per_device(): far = lax.all_to_all(far, 'lo', 0, 0, tiled=True)]
    ppermute x1, waiting for transfers between devices: 5.32 us -> 0.01 us  [per_device(): far_table = lax.ppermute(table, 'hi', [(0, 1), (1, 0)])]
    all_to_all x1, waiting for transfers between devices: 0.44 us -> 5.53 us  [per_device(): near = lax.all_to_all(near, 'lo', 0, 0, tiled=True)]
    pallas_call x5 -> x7, Pallas kernels: 50.4 us -> 55 us  [the longest x2 17.1 us: left_products(): pl.pallas_call(functools.partial(left_kernel, base, total), in_specs=[pl....]
    all_to_all x1, starting transfers between devices: 7.49 us -> 3.92 us  [per_device(): far = lax.all_to_all(far, 'lo', 0, 0, tiled=True)]
    unnamed x9 -> x7, local copies, waits for them, and re-layouts: 2.42 us -> 2.43 us
  transfers between devices with their start and end apart: 4 -> 4, of which waited for: 3 -> 2; matrix products, arithmetic and copies ran while one was open for 1% -> 1% of each run, Pallas kernels for 40% -> 53%
where the time goes in v3:
time: 96.1 us; the launch traced here: 95.6 us
  Pallas kernels  66.8 us (70%)
  starting transfers between devices  18 us (19%)
  waiting for transfers between devices  6.17 us (6%)
  local copies, waits for them, and re-layouts  3.05 us (3%)
    pallas_call x2, Pallas kernels, left_products(): pl.pallas_call(functools.partial(left_kernel, base, total), in_specs=[pl....  17.1 us
    pallas_call x1, Pallas kernels, close(): pl.pallas_call(functools.partial(close_kernel, caps), in_specs=[smem] * 3...  15.9 us
    pallas_call x1, Pallas kernels, factor(): pl.pallas_call(factor_kernel, in_specs=[hbm, hbm], out_specs=(vmem, hbm,...  11.8 us
    pallas_call x1, Pallas kernels, bases(): pl.pallas_call(basis_kernel, in_specs=[hbm, hbm, vmem, hbm, vmem], out_sp...  10.5 us
    pallas_call x1, Pallas kernels, unpack_near(): pl.pallas_call(functools.partial(unpack_kernel, caps), in_specs=[pl.Block...  6.32 us
    all_to_all x1, starting transfers between devices, per_device(): wanted = lax.all_to_all(wanted, 'lo', 0, 0, tiled=True)  6.29 us
    all_to_all x1, waiting for transfers between devices, per_device(): near = lax.all_to_all(near, 'lo', 0, 0, tiled=True)  5.53 us
    pallas_call x2, Pallas kernels, gather(): pl.pallas_call(functools.partial(gather_kernel, picks, sizes, far), in_sp...  5.21 us
  transfers between devices with their start and end apart: 4, of which 2 were waited for; matrix products, arithmetic and copies ran while one was open for 1% of the time, Pallas kernels for 53%

profile of v3, /device:TPU:0, one launch (start us, length us, event | category | flops | bytes accessed | tf_op | source)
XLA Modules:
  0.0 95.6 jit_solution(15515401959399936695)
XLA Ops:
  0.6 0.7 pad_add_fusion
  1.3 0.6 broadcast.3
  1.9 6.3 %all-to-all-start = ((s32[16,1,256]{2,1,0:T(1,128)}), s32[16,1,256]{2,1,0:T(1,128)S(1)}, u32[]{:S(2)}, u32[]{:S(2)}) async-start(s32[16,1,256]{2,1,0:T(1,128)} %broadcast.3), calls=%async_computation | async-start | bytes 32768 | tf_op jit(solution)/shard_map/all_to_all | solution.py:436
  8.2 11.8 %factor.1 = (f32[18,48,128]{2,1,0:T(8,128)}, f32[64,64,128]{2,1,0:T(8,128)}, f32[64,128]{1,0:T(8,128)}) custom-call(f32[32,64,128]{2,1,0:T(8,128)} %u_hbm.3, f32[16,64,128]{2,1,0:T(8,128)} %e_hbm.3), custom_call_target="tpu_custom_call" | custom-call | flops 12650000384 | tf_op jit(solution)/shard_map/factor/pallas_call | solution.py:124
  20.0 2.7 %collective-permute-start = (f32[18,48,128]{2,1,0:T(8,128)}, f32[18,48,128]{2,1,0:T(8,128)S(1)}, u32[]{:S(2)}, u32[]{:S(2)}) collective-permute-start(f32[18,48,128]{2,1,0:T(8,128)} %get-tuple-element.16.table_ref), channel_id=1, source_target_pairs={{0,16},{16,0},{1,17},{17,1},{2,18},{18,2},{3,19},{19,3},{4,20},{20... | collective-permute-start | bytes 1327112 | tf_op jit(solution)/shard_map/ppermute | solution.py:438
  22.7 0.0 all-to-all-done
  22.7 0.6 copy.17
  23.3 2.6 %gather.2 = f32[2304,128]{1,0:T(8,128)} custom-call(s32[16,256]{1,0:T(8,128)} %bitcast.17, f32[18,48,128]{2,1,0:T(8,128)} %get-tuple-element.16.table_ref), custom_call_target="tpu_custom_call" | custom-call | flops 115000000 | tf_op jit(solution)/shard_map/gather/pallas_call | solution.py:332
  25.9 5.1 %all-to-all-start.1 = ((f32[16,144,128]{2,1,0:T(8,128)}), f32[16,144,128]{2,1,0:T(8,128)S(1)}, u32[]{:S(2)}, u32[]{:S(2)}) async-start(f32[16,144,128]{2,1,0:T(8,128)} %bitcast.11), calls=%async_computation.1 | async-start | bytes 2359296 | tf_op jit(solution)/shard_map/all_to_all | solution.py:443
  31.0 8.6 %left.3.pp_hbm = bf16[256,64,128]{2,1,0:T(8,128)(2,1)} custom-call(s32[256]{0:T(256)} %rows_ref.3, f32[864,128]{1,0:T(8,128)} %bitcast.14, f32[64,64,256]{2,1,0:T(8,128)} %s_hbm.3), custom_call_target="tpu_custom_call" | custom-call | flops 46000001024 | tf_op jit(solution)/shard_map/left/pallas_call | solution.py:194
  39.6 8.5 %left.2.lp_hbm = bf16[256,64,128]{2,1,0:T(8,128)(2,1)} custom-call(s32[256]{0:T(256)} %rows_ref.2, f32[864,128]{1,0:T(8,128)} %bitcast.15, f32[64,64,256]{2,1,0:T(8,128)} %s_hbm.2), custom_call_target="tpu_custom_call" | custom-call | flops 46000001024 | tf_op jit(solution)/shard_map/left/pallas_call | solution.py:194
  48.1 0.0 collective-permute-done.table_ref
  48.1 0.0 copy-start.2
  48.1 0.8 copy-done.2
  48.9 2.6 %gather.3 = f32[2304,128]{1,0:T(8,128)} custom-call(s32[16,256]{1,0:T(8,128)} %bitcast.18, f32[18,48,128]{2,1,0:T(8,128)} %copy-done.2), custom_call_target="tpu_custom_call" | custom-call | flops 115000000 | tf_op jit(solution)/shard_map/gather/pallas_call | solution.py:332
  51.5 5.5 %all-to-all-done.1 = f32[16,144,128]{2,1,0:T(8,128)S(1)} async-done(((f32[16,144,128]{2,1,0:T(8,128)}), f32[16,144,128]{2,1,0:T(8,128)S(1)}, u32[]{:S(2)}, u32[]{:S(2)}) %all-to-all-start.1) | async-done | bytes 1179680 | tf_op jit(solution)/shard_map/all_to_all | solution.py:443
  57.0 0.0 copy-start
  57.0 3.9 %all-to-all-start.2 = ((f32[16,144,128]{2,1,0:T(8,128)}), f32[16,144,128]{2,1,0:T(8,128)S(1)}, u32[]{:S(2)}, u32[]{:S(2)}) async-start(f32[16,144,128]{2,1,0:T(8,128)} %bitcast.10), calls=%async_computation.2 | async-start | bytes 2359296 | tf_op jit(solution)/shard_map/all_to_all | solution.py:450
  60.9 10.5 %basis.1 = (f32[32,64,128]{2,1,0:T(8,128)}, f32[16,64,128]{2,1,0:T(8,128)}) custom-call(f32[32,64,128]{2,1,0:T(8,128)} %u_hbm.3, f32[16,64,128]{2,1,0:T(8,128)} %e_hbm.3, f32[864,128]{1,0:T(8,128)} %bitcast.16, f32[64,64,128]{2,1,0:T(8,128)} %get-tuple-element.19.r_hbm, f32[64,128]{1,0:T(8,128)} %get-tuple-element.20.rinv_ref), custom_call_target="tpu_custom_call" | custom-call | flops 10350000128 | tf_op jit(solution)/shard_map/basis/pallas_call | solution.py:417
  71.5 0.0 copy-done
  71.5 6.3 %unpack.1.near_hbm = bf16[128,64,256]{2,1,0:T(8,128)(2,1)} custom-call(f32[2304,128]{1,0:T(8,128)} %bitcast.12), custom_call_target="tpu_custom_call" | custom-call | flops 5750000128 | tf_op jit(solution)/shard_map/unpack/pallas_call | solution.py:220
  77.8 0.6 all-to-all-done.2
  78.4 0.0 copy-start.1
  78.4 1.1 %copy-done.1 = f32[16,144,128]{2,1,0:T(8,128)} copy-done((f32[16,144,128]{2,1,0:T(8,128)}, f32[16,144,128]{2,1,0:T(8,128)S(1)}, u32[]{:S(2)}) %copy-start.1) | copy-done | bytes 1179672
  79.5 15.9 %close.1 = (f32[64,64,256]{2,1,0:T(8,128)}, f32[64,64,256]{2,1,0:T(8,128)}) custom-call(s32[256]{0:T(256)} %lslots_ref.1, s32[256]{0:T(256)} %pslots_ref.1, s32[1,2]{1,0:T(1,128)} %count_ref.1, bf16[128,64,256]{2,1,0:T(8,128)(2,1)} %unpack.1.near_hbm, f32[2304,128]{1,0:T(8,128)} %bitcast.13, bf16[256,64,128]{2,1,0:T(8,128)(2,1)} %left.2.lp_hbm, ...), custom_call_target="tpu_custom_call" | custom-call | flops 21849999360 | tf_op jit(solution)/shard_map/close/pallas_call | solution.py:293
Async XLA Ops:
  1.9 20.7 %all-to-all-start = ((s32[16,1,256]{2,1,0:T(1,128)}), s32[16,1,256]{2,1,0:T(1,128)S(1)}, u32[]{:S(2)}, u32[]{:S(2)}) async-start(s32[16,1,256]{2,1,0:T(1,128)} %broadcast.3), calls=%async_computation | async-start | bytes 32768 | tf_op jit(solution)/shard_map/all_to_all | solution.py:436
  20.0 28.1 %collective-permute-start = (f32[18,48,128]{2,1,0:T(8,128)}, f32[18,48,128]{2,1,0:T(8,128)S(1)}, u32[]{:S(2)}, u32[]{:S(2)}) collective-permute-start(f32[18,48,128]{2,1,0:T(8,128)} %get-tuple-element.16.table_ref), channel_id=1, source_target_pairs={{0,16},{16,0},{1,17},{17,1},{2,18},{18,2},{3,19},{19,3},{4,20},{20... | collective-permute-start | bytes 1327112 | tf_op jit(solution)/shard_map/ppermute | solution.py:438
  25.9 31.2 %all-to-all-start.1 = ((f32[16,144,128]{2,1,0:T(8,128)}), f32[16,144,128]{2,1,0:T(8,128)S(1)}, u32[]{:S(2)}, u32[]{:S(2)}) async-start(f32[16,144,128]{2,1,0:T(8,128)} %bitcast.11), calls=%async_computation.1 | async-start | bytes 2359296 | tf_op jit(solution)/shard_map/all_to_all | solution.py:443
  48.1 0.8 copy-start.2
  57.0 14.5 %copy-start = (f32[16,144,128]{2,1,0:T(8,128)}, f32[16,144,128]{2,1,0:T(8,128)S(1)}, u32[]{:S(2)}) copy-start(f32[16,144,128]{2,1,0:T(8,128)S(1)} %all-to-all-done.1) | copy-start | bytes 3538948
  57.0 21.4 %all-to-all-start.2 = ((f32[16,144,128]{2,1,0:T(8,128)}), f32[16,144,128]{2,1,0:T(8,128)S(1)}, u32[]{:S(2)}, u32[]{:S(2)}) async-start(f32[16,144,128]{2,1,0:T(8,128)} %bitcast.10), calls=%async_computation.2 | async-start | bytes 2359296 | tf_op jit(solution)/shard_map/all_to_all | solution.py:450
  78.4 1.1 %copy-start.1 = (f32[16,144,128]{2,1,0:T(8,128)}, f32[16,144,128]{2,1,0:T(8,128)S(1)}, u32[]{:S(2)}) copy-start(f32[16,144,128]{2,1,0:T(8,128)S(1)} %all-to-all-done.2) | copy-start | bytes 3538948

commit v4 on v3

--- a/solution.py
+++ b/solution.py
@@ -32,10 +32,20 @@
     hi = x.astype(BF16)
     return hi, (x - hi.astype(F32)).astype(BF16)
 
+def split3(x):
+    h = x.astype(BF16)
+    r = x - h.astype(F32)
+    m = r.astype(BF16)
+    return h, m, (r - m.astype(F32)).astype(BF16)
+
+def stack3(x):
+    h, m, w = split3(x)
+    return jnp.concatenate([h,h,m,m,w,h], 0)
+
 def factor_kernel(u_hbm, e_hbm, table_ref, r_hbm, rinv_ref, nat, gd, a_ref, u_ref, e_ref, r_ref, usem, esem, rsem):
     L = u_ref.shape[0]; Pn = e_ref.shape[0]; C = L+Pn
-    part = L//4
-    u_in = [pltpu.make_async_copy(u_hbm.at[pl.ds(i*part, part)], u_ref.at[pl.ds(i*part, part)], usem.at[i]) for i in range(4)]
+    part = L//2
+    u_in = [pltpu.make_async_copy(u_hbm.at[pl.ds(i*part, part)], u_ref.at[pl.ds(i*part, part)], usem.at[i]) for i in range(2)]
     e_in = pltpu.make_async_copy(e_hbm, e_ref, esem)
     r_out = [pltpu.make_async_copy(r_ref.at[pl.ds(8*p, 8)], r_hbm.at[pl.ds(8*p, 8)], rsem.at[p]) for p in range(8)]
     for copy in u_in + [e_in]:
@@ -45,11 +55,13 @@
     left32 = left[:32]
     def gram(l, c):
         u = u_ref[l]
-        g = lax.dot_general(u, jnp.concatenate([u,u],0), NT, precision=HI, preferred_element_type=F32)
+        h, m, w = split3(u)
+        rows = jnp.concatenate([h,h,m,m,w,h], 1)
+        g = lax.dot_general(jnp.concatenate([h,m,h,m,h,w], 1), jnp.concatenate([rows,rows],0), NT, preferred_element_type=F32)
         gd[l] = g
         nat[pl.ds(l*40,32),:] = jnp.where(left32, g[:32], g[32:])
         return c
-    for i in range(4):
+    for i in range(2):
         u_in[i].wait()
         lax.fori_loop(i*part, (i+1)*part, gram, 0, unroll=part)
     e_in.wait()
@@ -57,10 +69,15 @@
         e = e_ref[p]
         er = pltpu.roll(e, 64, 1)
         e0 = jnp.where(left, e, er); e1 = jnp.where(left, er, e)
-        t0 = lax.dot_general(gd[2*p][:, :64], e0, NN, precision=HI, preferred_element_type=F32)
-        t1 = lax.dot_general(gd[2*p+1][:, :64], e1, NN, precision=HI, preferred_element_type=F32)
+        def times(g, x):
+            h, m, w = (y.astype(F32) for y in split3(g))
+            hm, hw = jnp.where(left, h, m).astype(BF16), jnp.where(left, h, w).astype(BF16)
+            return lax.dot_general(jnp.concatenate([hm,hm,hw], 1), stack3(x), NN, preferred_element_type=F32)
+        t0 = times(gd[2*p], e0)
+        t1 = times(gd[2*p+1], e1)
         est = jnp.concatenate([e0,e1],0).T[:64]
-        g = lax.dot_general(est, jnp.concatenate([t0,t1],0), NN, precision=HI, preferred_element_type=F32)
+        h, m, w = split3(est)
+        g = lax.dot_general(jnp.concatenate([h,m,h,m,h,w], 1), stack3(jnp.concatenate([t0,t1],0)), NN, preferred_element_type=F32)
         nat[pl.ds((L+p)*40,32),:] = jnp.where(left32, g[:32], g[32:])
         return c
     lax.fori_loop(0, Pn, parent, 0, unroll=16)
@@ -125,7 +142,7 @@
         in_specs=[hbm, hbm], out_specs=(vmem, hbm, vmem),
         out_shape=(jax.ShapeDtypeStruct((18,C,128),F32), jax.ShapeDtypeStruct((64,64,128),F32), jax.ShapeDtypeStruct((64,128),F32)),
         scratch_shapes=[pltpu.VMEM((C*40,128),F32), pltpu.VMEM((L,64,128),F32), pltpu.VMEM((64,64,128),F32),
-                        pltpu.VMEM(u.shape,F32), pltpu.VMEM(e.shape,F32), pltpu.VMEM((64,64,128),F32), dma((4,)), dma, dma((8,))],
+                        pltpu.VMEM(u.shape,F32), pltpu.VMEM(e.shape,F32), pltpu.VMEM((64,64,128),F32), dma((2,)), dma, dma((8,))],
         **params(11, 60),
         name="factor")(u, e)
 
@@ -180,7 +197,7 @@
             res = lax.dot_general(jnp.concatenate([a, a], 1), jnp.concatenate([hi,hi,lo,lo], 0), NN, preferred_element_type=F32)
             p_ref[g, b] = mix(res)
             return _
-        lax.fori_loop(0, 128, one, 0, unroll=64)
+        lax.fori_loop(0, 128, one, 0, unroll=128)
         p_out[g].start()
     for copy in p_out:
         copy.wait()
@@ -268,7 +285,7 @@
             res = lax.dot_general(jnp.concatenate([a, a], 1), w, NT, preferred_element_type=F32)
             c_ref[pl.ds(pl.multiple_of(b*40, 8), 32), :] = jnp.concatenate([res[:32], res[32:]], 1)
             return _
-        lax.fori_loop(0, 128, one, 0, unroll=64)
+        lax.fori_loop(0, 128, one, 0, unroll=128)
         live = lane + start < jnp.where(low, count_ref[0, 0], count_ref[0, 1])
         for i in range(32):
             x = c_ref[pl.ds(i, 128, 40), :].T
@@ -296,7 +313,7 @@
         scratch_shapes=[pltpu.VMEM((n,128,64,128),BF16),
                         pltpu.VMEM((n,64,64,128),F32), pltpu.VMEM((128*40,128),F32), pltpu.VMEM((total,64,256),BF16),
                         dma((2,)), dma((n,)), dma((n,))],
-        **params(19, 60), name="close")(lslots, pslots, counts, near, far, lprods, pprods)
+        **params(19, 51), name="close")(lslots, pslots, counts, near, far, lprods, pprods)
 
 def gather_kernel(picks, sizes, far, idx_ref, table_ref, out_ref):
     peers, wide = idx_ref.shape[0], len(picks)
@@ -332,7 +349,7 @@
     return pl.pallas_call(functools.partial(gather_kernel, picks, sizes, far),
         in_specs=[vmem, vmem], out_specs=vmem,
         out_shape=jax.ShapeDtypeStruct((peers*18*wide,128),F32),
-        **params(0.1, 60), name="gather")(idx, table)
+        **params(2, 16), name="gather")(idx, table)
 
 def basis_kernel(u_hbm, e_hbm, table_ref, r_hbm, rinv_ref, basis_hbm, nt_hbm, x_ref, nat, u_ref, e_ref, r_ref, basis_ref, nt_ref, rsem, sem):
     L = u_ref.shape[0]; Pn = e_ref.shape[0]; C = L+Pn

time: 96.1 us -> 91.9 us (0.956)
  Pallas kernels: 66.8 us -> 62.2 us
  waiting for transfers between devices: 6.17 us -> 7.88 us
  local copies, waits for them, and re-layouts: 3.05 us -> 1.68 us
    pallas_call x2, Pallas kernels: 5.21 us -> 3.17 us  [gather(): pl.pallas_call(functools.partial(gather_kernel, picks, sizes, far), in_sp...]
    all_to_all x1, waiting for transfers between devices: 5.53 us -> 7.28 us  [per_device(): near = lax.all_to_all(near, 'lo', 0, 0, tiled=True)]
    pallas_call x1, Pallas kernels: 15.9 us -> 14.2 us  [close(): pl.pallas_call(functools.partial(close_kernel, caps), in_specs=[smem] * 3...]
    unnamed x7 -> x11, local copies, waits for them, and re-layouts: 2.43 us -> 1.07 us
  transfers between devices with their start and end apart: 4 -> 4, of which waited for: 2 -> 2; matrix products, arithmetic and copies ran while one was open for 1% -> 0% of each run, Pallas kernels for 53% -> 53%
where the time goes in v4:
time: 91.9 us; the launch traced here: 91.4 us
  Pallas kernels  62.2 us (68%)
  starting transfers between devices  18 us (20%)
  waiting for transfers between devices  7.88 us (9%)
  local copies, waits for them, and re-layouts  1.68 us (2%)
  between operations  0.92 us (1%)
    pallas_call x2, Pallas kernels, left_products(): pl.pallas_call(functools.partial(left_kernel, base, total), in_specs=[pl....  17.1 us
    pallas_call x1, Pallas kernels, close(): pl.pallas_call(functools.partial(close_kernel, caps), in_specs=[smem] * 3...  14.2 us
    pallas_call x1, Pallas kernels, factor(): pl.pallas_call(factor_kernel, in_specs=[hbm, hbm], out_specs=(vmem, hbm,...  10.9 us
    pallas_call x1, Pallas kernels, bases(): pl.pallas_call(basis_kernel, in_specs=[hbm, hbm, vmem, hbm, vmem], out_sp...  10.5 us
    all_to_all x1, waiting for transfers between devices, per_device(): near = lax.all_to_all(near, 'lo', 0, 0, tiled=True)  7.28 us
    pallas_call x1, Pallas kernels, unpack_near(): pl.pallas_call(functools.partial(unpack_kernel, caps), in_specs=[pl.Block...  6.34 us
    all_to_all x1, starting transfers between devices, per_device(): wanted = lax.all_to_all(wanted, 'lo', 0, 0, tiled=True)  6.29 us
    all_to_all x1, starting transfers between devices, per_device(): near = lax.all_to_all(near, 'lo', 0, 0, tiled=True)  5.12 us
  transfers between devices with their start and end apart: 4, of which 2 were waited for; matrix products, arithmetic and copies ran while one was open for 0% of the time, Pallas kernels for 53%

profile of v4, /device:TPU:0, one launch (start us, length us, event | category | flops | bytes accessed | tf_op | source)
XLA Modules:
  0.0 91.4 jit_solution(15620421359187200777)
XLA Ops:
  0.6 0.7 pad_add_fusion
  1.3 0.6 broadcast.3
  1.9 6.3 %all-to-all-start = ((s32[16,1,256]{2,1,0:T(1,128)}), s32[16,1,256]{2,1,0:T(1,128)S(1)}, u32[]{:S(2)}, u32[]{:S(2)}) async-start(s32[16,1,256]{2,1,0:T(1,128)} %broadcast.3), calls=%async_computation | async-start | bytes 32768 | tf_op jit(solution)/shard_map/all_to_all | solution.py:453
  8.2 10.9 %factor.1 = (f32[18,48,128]{2,1,0:T(8,128)}, f32[64,64,128]{2,1,0:T(8,128)}, f32[64,128]{1,0:T(8,128)}) custom-call(f32[32,64,128]{2,1,0:T(8,128)} %u_hbm.3, f32[16,64,128]{2,1,0:T(8,128)} %e_hbm.3), custom_call_target="tpu_custom_call" | custom-call | flops 12650000384 | tf_op jit(solution)/shard_map/factor/pallas_call | solution.py:141
  19.1 2.7 %collective-permute-start = (f32[18,48,128]{2,1,0:T(8,128)}, f32[18,48,128]{2,1,0:T(8,128)S(1)}, u32[]{:S(2)}, u32[]{:S(2)}) collective-permute-start(f32[18,48,128]{2,1,0:T(8,128)} %get-tuple-element.16.table_ref), channel_id=1, source_target_pairs={{0,16},{16,0},{1,17},{17,1},{2,18},{18,2},{3,19},{19,3},{4,20},{20... | collective-permute-start | bytes 1327112 | tf_op jit(solution)/shard_map/ppermute | solution.py:455
  21.8 0.0 all-to-all-done
  21.8 0.0 copy-start
  21.8 1.0 %copy-done = f32[18,48,128]{2,1,0:T(8,128)S(1)} copy-done((f32[18,48,128]{2,1,0:T(8,128)S(1)}, f32[18,48,128]{2,1,0:T(8,128)}, u32[]{:S(2)}) %copy-start) | copy-done | bytes 442392
  22.8 1.5 %gather.2 = f32[2304,128]{1,0:T(8,128)} custom-call(s32[16,256]{1,0:T(8,128)S(1)} %bitcast.11, f32[18,48,128]{2,1,0:T(8,128)S(1)} %copy-done), custom_call_target="tpu_custom_call" | custom-call | flops 2300000000 | tf_op jit(solution)/shard_map/gather/pallas_call | solution.py:349
  24.4 5.1 %all-to-all-start.1 = ((f32[16,144,128]{2,1,0:T(8,128)}), f32[16,144,128]{2,1,0:T(8,128)S(1)}, u32[]{:S(2)}, u32[]{:S(2)}) async-start(f32[16,144,128]{2,1,0:T(8,128)} %bitcast.3), calls=%async_computation.1 | async-start | bytes 2359296 | tf_op jit(solution)/shard_map/all_to_all | solution.py:460
  29.5 8.6 %left.3.pp_hbm = bf16[256,64,128]{2,1,0:T(8,128)(2,1)} custom-call(s32[256]{0:T(256)} %rows_ref.3, f32[864,128]{1,0:T(8,128)} %bitcast.13, f32[64,64,256]{2,1,0:T(8,128)} %s_hbm.3), custom_call_target="tpu_custom_call" | custom-call | flops 46000001024 | tf_op jit(solution)/shard_map/left/pallas_call | solution.py:211
  38.1 8.5 %left.2.lp_hbm = bf16[256,64,128]{2,1,0:T(8,128)(2,1)} custom-call(s32[256]{0:T(256)} %rows_ref.2, f32[864,128]{1,0:T(8,128)} %bitcast.14, f32[64,64,256]{2,1,0:T(8,128)} %s_hbm.2), custom_call_target="tpu_custom_call" | custom-call | flops 46000001024 | tf_op jit(solution)/shard_map/left/pallas_call | solution.py:211
  46.6 0.0 collective-permute-done.table_ref
  46.6 1.6 %gather.3 = f32[2304,128]{1,0:T(8,128)} custom-call(s32[16,256]{1,0:T(8,128)S(1)} %bitcast.12, f32[18,48,128]{2,1,0:T(8,128)S(1)} %collective-permute-done.table_ref), custom_call_target="tpu_custom_call" | custom-call | flops 2300000000 | tf_op jit(solution)/shard_map/gather/pallas_call | solution.py:349
  48.3 7.3 %all-to-all-done.1 = f32[16,144,128]{2,1,0:T(8,128)S(1)} async-done(((f32[16,144,128]{2,1,0:T(8,128)}), f32[16,144,128]{2,1,0:T(8,128)S(1)}, u32[]{:S(2)}, u32[]{:S(2)}) %all-to-all-start.1) | async-done | bytes 1179680 | tf_op jit(solution)/shard_map/all_to_all | solution.py:460
  55.6 0.0 copy-start.4
  55.6 3.9 %all-to-all-start.2 = ((f32[16,144,128]{2,1,0:T(8,128)}), f32[16,144,128]{2,1,0:T(8,128)S(1)}, u32[]{:S(2)}, u32[]{:S(2)}) async-start(f32[16,144,128]{2,1,0:T(8,128)} %bitcast.5), calls=%async_computation.2 | async-start | bytes 2359296 | tf_op jit(solution)/shard_map/all_to_all | solution.py:467
  59.5 10.5 %basis.1 = (f32[32,64,128]{2,1,0:T(8,128)}, f32[16,64,128]{2,1,0:T(8,128)}) custom-call(f32[32,64,128]{2,1,0:T(8,128)} %u_hbm.3, f32[16,64,128]{2,1,0:T(8,128)} %e_hbm.3, f32[864,128]{1,0:T(8,128)} %bitcast.15, f32[64,64,128]{2,1,0:T(8,128)} %get-tuple-element.19.r_hbm, f32[64,128]{1,0:T(8,128)} %get-tuple-element.20.rinv_ref), custom_call_target="tpu_custom_call" | custom-call | flops 10350000128 | tf_op jit(solution)/shard_map/basis/pallas_call | solution.py:434
  70.0 0.0 copy-done.4
  70.0 0.0 copy-start.1
  70.0 0.0 copy-start.2
  70.0 0.0 copy-start.3
  70.0 6.3 %unpack.1.near_hbm = bf16[128,64,256]{2,1,0:T(8,128)(2,1)} custom-call(f32[2304,128]{1,0:T(8,128)} %bitcast.16), custom_call_target="tpu_custom_call" | custom-call | flops 5750000128 | tf_op jit(solution)/shard_map/unpack/pallas_call | solution.py:237
  76.4 0.6 all-to-all-done.2
  77.0 0.0 copy-done.1
  77.0 0.0 copy-done.2
  77.0 0.0 copy-done.3
  77.0 14.2 %close.1 = (f32[64,64,256]{2,1,0:T(8,128)}, f32[64,64,256]{2,1,0:T(8,128)}) custom-call(s32[256]{0:T(256)S(1)} %copy-done.1, s32[256]{0:T(256)S(1)} %copy-done.2, s32[1,2]{1,0:T(1,128)S(1)} %copy-done.3, bf16[128,64,256]{2,1,0:T(8,128)(2,1)} %unpack.1.near_hbm, f32[2304,128]{1,0:T(8,128)S(1)} %bitcast.10, bf16[256,64,128]{2,1,0:T(8,128)(2,1)} %left.2.lp_hbm, ...), custom_call_target="tpu_custom_call" | custom-call | flops 21849999360 | tf_op jit(solution)/shard_map/close/pallas_call | solution.py:310
  (1 shorter events, 0.0 us)
Async XLA Ops:
  1.9 19.9 %all-to-all-start = ((s32[16,1,256]{2,1,0:T(1,128)}), s32[16,1,256]{2,1,0:T(1,128)S(1)}, u32[]{:S(2)}, u32[]{:S(2)}) async-start(s32[16,1,256]{2,1,0:T(1,128)} %broadcast.3), calls=%async_computation | async-start | bytes 32768 | tf_op jit(solution)/shard_map/all_to_all | solution.py:453
  19.1 27.5 %collective-permute-start = (f32[18,48,128]{2,1,0:T(8,128)}, f32[18,48,128]{2,1,0:T(8,128)S(1)}, u32[]{:S(2)}, u32[]{:S(2)}) collective-permute-start(f32[18,48,128]{2,1,0:T(8,128)} %get-tuple-element.16.table_ref), channel_id=1, source_target_pairs={{0,16},{16,0},{1,17},{17,1},{2,18},{18,2},{3,19},{19,3},{4,20},{20... | collective-permute-start | bytes 1327112 | tf_op jit(solution)/shard_map/ppermute | solution.py:455
  21.8 1.0 %copy-start = (f32[18,48,128]{2,1,0:T(8,128)S(1)}, f32[18,48,128]{2,1,0:T(8,128)}, u32[]{:S(2)}) copy-start(f32[18,48,128]{2,1,0:T(8,128)} %get-tuple-element.16.table_ref) | copy-start | bytes 1327108
  24.4 31.2 %all-to-all-start.1 = ((f32[16,144,128]{2,1,0:T(8,128)}), f32[16,144,128]{2,1,0:T(8,128)S(1)}, u32[]{:S(2)}, u32[]{:S(2)}) async-start(f32[16,144,128]{2,1,0:T(8,128)} %bitcast.3), calls=%async_computation.1 | async-start | bytes 2359296 | tf_op jit(solution)/shard_map/all_to_all | solution.py:460
  55.6 14.4 %copy-start.4 = (f32[16,144,128]{2,1,0:T(8,128)}, f32[16,144,128]{2,1,0:T(8,128)S(1)}, u32[]{:S(2)}) copy-start(f32[16,144,128]{2,1,0:T(8,128)S(1)} %all-to-all-done.1) | copy-start | bytes 3538948
  55.6 21.4 %all-to-all-start.2 = ((f32[16,144,128]{2,1,0:T(8,128)}), f32[16,144,128]{2,1,0:T(8,128)S(1)}, u32[]{:S(2)}, u32[]{:S(2)}) async-start(f32[16,144,128]{2,1,0:T(8,128)} %bitcast.5), calls=%async_computation.2 | async-start | bytes 2359296 | tf_op jit(solution)/shard_map/all_to_all | solution.py:467
  70.0 7.0 %copy-start.1 = (s32[256]{0:T(256)S(1)}, s32[256]{0:T(256)}, u32[]{:S(2)}) copy-start(s32[256]{0:T(256)} %lslots_ref.1) | copy-start | bytes 3076
  70.0 7.0 %copy-start.2 = (s32[256]{0:T(256)S(1)}, s32[256]{0:T(256)}, u32[]{:S(2)}) copy-start(s32[256]{0:T(256)} %pslots_ref.1) | copy-start | bytes 3076
  70.0 7.0 %copy-start.3 = (s32[1,2]{1,0:T(1,128)S(1)}, s32[1,2]{1,0:T(1,128)}, u32[]{:S(2)}) copy-start(s32[1,2]{1,0:T(1,128)} %count_ref.1) | copy-start | bytes 28

commit v5 on v4

--- a/solution.py
+++ b/solution.py
@@ -253,9 +253,10 @@
     def p_in(g):
         src, i = (lp_hbm, g) if g < chunks else (pp_hbm, g - chunks)
         return pltpu.make_async_copy(src.at[pl.ds(i*128, 128)], p_ref.at[g], psem.at[g])
-    def out(g):
+    def out(g, part):
         dst, i = (lout_hbm, g) if g < chunks else (pout_hbm, g - chunks)
-        return pltpu.make_async_copy(out_ref.at[g], dst.at[:, :, pl.ds(i*128, 128)], osem.at[g])
+        rows = pl.ds(16*part, 16)
+        return pltpu.make_async_copy(out_ref.at[g, rows], dst.at[rows, :, pl.ds(i*128, 128)], osem.at[g, part])
     for g in range(chunks):
         p_in(g).start()
     for copy in w_in:
@@ -287,18 +288,21 @@
             return _
         lax.fori_loop(0, 128, one, 0, unroll=128)
         live = lane + start < jnp.where(low, count_ref[0, 0], count_ref[0, 1])
-        for i in range(32):
-            x = c_ref[pl.ds(i, 128, 40), :].T
-            out_ref[g, i] = jnp.where(live, x[:64], 0.0)
-            out_ref[g, i+32] = jnp.where(live, x[64:], 0.0)
-        for i in range(2*chunks):
-            @pl.when(g == i)
-            def _():
-                out(i).start()
+        for half in range(2):
+            for i in range(16*half, 16*half + 16):
+                x = c_ref[pl.ds(i, 128, 40), :].T
+                out_ref[g, i] = jnp.where(live, x[:64], 0.0)
+                out_ref[g, i+32] = jnp.where(live, x[64:], 0.0)
+            for i in range(2*chunks):
+                @pl.when(g == i)
+                def _():
+                    out(i, half).start()
+                    out(i, half + 2).start()
         return carry
     lax.fori_loop(0, 2*chunks, chunk, 0)
     for g in range(2*chunks):
-        out(g).wait()
+        for part in range(4):
+            out(g, part).wait()
 
 def close(lslots, pslots, counts, near, far, lprods, pprods, caps):
     B = lprods.shape[0]
@@ -312,7 +316,7 @@
         out_shape=(jax.ShapeDtypeStruct((64,64,B), F32),)*2,
         scratch_shapes=[pltpu.VMEM((n,128,64,128),BF16),
                         pltpu.VMEM((n,64,64,128),F32), pltpu.VMEM((128*40,128),F32), pltpu.VMEM((total,64,256),BF16),
-                        dma((2,)), dma((n,)), dma((n,))],
+                        dma((2,)), dma((n,)), dma((n,4))],
         **params(19, 51), name="close")(lslots, pslots, counts, near, far, lprods, pprods)
 
 def gather_kernel(picks, sizes, far, idx_ref, table_ref, out_ref):

time: 91.9 us -> 91.7 us (level)
  no operation moved by 1% of the time
where the time goes in v5:
time: 91.7 us; the launch traced here: 91.2 us
  Pallas kernels  62.1 us (68%)
  starting transfers between devices  18 us (20%)
  waiting for transfers between devices  7.87 us (9%)
  local copies, waits for them, and re-layouts  1.68 us (2%)
  between operations  0.92 us (1%)
    pallas_call x2, Pallas kernels, left_products(): pl.pallas_call(functools.partial(left_kernel, base, total), in_specs=[pl....  17.1 us
    pallas_call x1, Pallas kernels, close(): pl.pallas_call(functools.partial(close_kernel, caps), in_specs=[smem] * 3...  14 us
    pallas_call x1, Pallas kernels, factor(): pl.pallas_call(factor_kernel, in_specs=[hbm, hbm], out_specs=(vmem, hbm,...  10.9 us
    pallas_call x1, Pallas kernels, bases(): pl.pallas_call(basis_kernel, in_specs=[hbm, hbm, vmem, hbm, vmem], out_sp...  10.5 us
    all_to_all x1, waiting for transfers between devices, per_device(): near = lax.all_to_all(near, 'lo', 0, 0, tiled=True)  7.27 us
    pallas_call x1, Pallas kernels, unpack_near(): pl.pallas_call(functools.partial(unpack_kernel, caps), in_specs=[pl.Block...  6.34 us
    all_to_all x1, starting transfers between devices, per_device(): wanted = lax.all_to_all(wanted, 'lo', 0, 0, tiled=True)  6.29 us
    all_to_all x1, starting transfers between devices, per_device(): near = lax.all_to_all(near, 'lo', 0, 0, tiled=True)  5.12 us
  transfers between devices with their start and end apart: 4, of which 2 were waited for; matrix products, arithmetic and copies ran while one was open for 0% of the time, Pallas kernels for 53%

profile of v5, /device:TPU:0, one launch (start us, length us, event | category | flops | bytes accessed | tf_op | source)
XLA Modules:
  0.0 91.2 jit_solution(1321945044883592706)
XLA Ops:
  0.6 0.7 pad_add_fusion
  1.3 0.6 broadcast.3
  1.9 6.3 %all-to-all-start = ((s32[16,1,256]{2,1,0:T(1,128)}), s32[16,1,256]{2,1,0:T(1,128)S(1)}, u32[]{:S(2)}, u32[]{:S(2)}) async-start(s32[16,1,256]{2,1,0:T(1,128)} %broadcast.3), calls=%async_computation | async-start | bytes 32768 | tf_op jit(solution)/shard_map/all_to_all | solution.py:457
  8.2 10.9 %factor.1 = (f32[18,48,128]{2,1,0:T(8,128)}, f32[64,64,128]{2,1,0:T(8,128)}, f32[64,128]{1,0:T(8,128)}) custom-call(f32[32,64,128]{2,1,0:T(8,128)} %u_hbm.3, f32[16,64,128]{2,1,0:T(8,128)} %e_hbm.3), custom_call_target="tpu_custom_call" | custom-call | flops 12650000384 | tf_op jit(solution)/shard_map/factor/pallas_call | solution.py:141
  19.1 2.7 %collective-permute-start = (f32[18,48,128]{2,1,0:T(8,128)}, f32[18,48,128]{2,1,0:T(8,128)S(1)}, u32[]{:S(2)}, u32[]{:S(2)}) collective-permute-start(f32[18,48,128]{2,1,0:T(8,128)} %get-tuple-element.16.table_ref), channel_id=1, source_target_pairs={{0,16},{16,0},{1,17},{17,1},{2,18},{18,2},{3,19},{19,3},{4,20},{20... | collective-permute-start | bytes 1327112 | tf_op jit(solution)/shard_map/ppermute | solution.py:459
  21.8 0.0 all-to-all-done
  21.8 0.0 copy-start
  21.8 1.0 %copy-done = f32[18,48,128]{2,1,0:T(8,128)S(1)} copy-done((f32[18,48,128]{2,1,0:T(8,128)S(1)}, f32[18,48,128]{2,1,0:T(8,128)}, u32[]{:S(2)}) %copy-start) | copy-done | bytes 442392
  22.8 1.5 %gather.2 = f32[2304,128]{1,0:T(8,128)} custom-call(s32[16,256]{1,0:T(8,128)S(1)} %bitcast.11, f32[18,48,128]{2,1,0:T(8,128)S(1)} %copy-done), custom_call_target="tpu_custom_call" | custom-call | flops 2300000000 | tf_op jit(solution)/shard_map/gather/pallas_call | solution.py:353
  24.4 5.1 %all-to-all-start.1 = ((f32[16,144,128]{2,1,0:T(8,128)}), f32[16,144,128]{2,1,0:T(8,128)S(1)}, u32[]{:S(2)}, u32[]{:S(2)}) async-start(f32[16,144,128]{2,1,0:T(8,128)} %bitcast.3), calls=%async_computation.1 | async-start | bytes 2359296 | tf_op jit(solution)/shard_map/all_to_all | solution.py:464
  29.5 8.6 %left.3.pp_hbm = bf16[256,64,128]{2,1,0:T(8,128)(2,1)} custom-call(s32[256]{0:T(256)} %rows_ref.3, f32[864,128]{1,0:T(8,128)} %bitcast.13, f32[64,64,256]{2,1,0:T(8,128)} %s_hbm.3), custom_call_target="tpu_custom_call" | custom-call | flops 46000001024 | tf_op jit(solution)/shard_map/left/pallas_call | solution.py:211
  38.1 8.5 %left.2.lp_hbm = bf16[256,64,128]{2,1,0:T(8,128)(2,1)} custom-call(s32[256]{0:T(256)} %rows_ref.2, f32[864,128]{1,0:T(8,128)} %bitcast.14, f32[64,64,256]{2,1,0:T(8,128)} %s_hbm.2), custom_call_target="tpu_custom_call" | custom-call | flops 46000001024 | tf_op jit(solution)/shard_map/left/pallas_call | solution.py:211
  46.6 0.0 collective-permute-done.table_ref
  46.7 1.6 %gather.3 = f32[2304,128]{1,0:T(8,128)} custom-call(s32[16,256]{1,0:T(8,128)S(1)} %bitcast.12, f32[18,48,128]{2,1,0:T(8,128)S(1)} %collective-permute-done.table_ref), custom_call_target="tpu_custom_call" | custom-call | flops 2300000000 | tf_op jit(solution)/shard_map/gather/pallas_call | solution.py:353
  48.3 7.3 %all-to-all-done.1 = f32[16,144,128]{2,1,0:T(8,128)S(1)} async-done(((f32[16,144,128]{2,1,0:T(8,128)}), f32[16,144,128]{2,1,0:T(8,128)S(1)}, u32[]{:S(2)}, u32[]{:S(2)}) %all-to-all-start.1) | async-done | bytes 1179680 | tf_op jit(solution)/shard_map/all_to_all | solution.py:464
  55.6 0.0 copy-start.4
  55.6 3.9 %all-to-all-start.2 = ((f32[16,144,128]{2,1,0:T(8,128)}), f32[16,144,128]{2,1,0:T(8,128)S(1)}, u32[]{:S(2)}, u32[]{:S(2)}) async-start(f32[16,144,128]{2,1,0:T(8,128)} %bitcast.5), calls=%async_computation.2 | async-start | bytes 2359296 | tf_op jit(solution)/shard_map/all_to_all | solution.py:471
  59.5 10.5 %basis.1 = (f32[32,64,128]{2,1,0:T(8,128)}, f32[16,64,128]{2,1,0:T(8,128)}) custom-call(f32[32,64,128]{2,1,0:T(8,128)} %u_hbm.3, f32[16,64,128]{2,1,0:T(8,128)} %e_hbm.3, f32[864,128]{1,0:T(8,128)} %bitcast.15, f32[64,64,128]{2,1,0:T(8,128)} %get-tuple-element.19.r_hbm, f32[64,128]{1,0:T(8,128)} %get-tuple-element.20.rinv_ref), custom_call_target="tpu_custom_call" | custom-call | flops 10350000128 | tf_op jit(solution)/shard_map/basis/pallas_call | solution.py:438
  70.0 0.0 copy-done.4
  70.0 0.0 copy-start.1
  70.0 0.0 copy-start.2
  70.0 0.0 copy-start.3
  70.0 6.3 %unpack.1.near_hbm = bf16[128,64,256]{2,1,0:T(8,128)(2,1)} custom-call(f32[2304,128]{1,0:T(8,128)} %bitcast.16), custom_call_target="tpu_custom_call" | custom-call | flops 5750000128 | tf_op jit(solution)/shard_map/unpack/pallas_call | solution.py:237
  76.4 0.6 all-to-all-done.2
  77.0 0.0 copy-done.1
  77.0 0.0 copy-done.2
  77.0 0.0 copy-done.3
  77.0 14.0 %close.1 = (f32[64,64,256]{2,1,0:T(8,128)}, f32[64,64,256]{2,1,0:T(8,128)}) custom-call(s32[256]{0:T(256)S(1)} %copy-done.1, s32[256]{0:T(256)S(1)} %copy-done.2, s32[1,2]{1,0:T(1,128)S(1)} %copy-done.3, bf16[128,64,256]{2,1,0:T(8,128)(2,1)} %unpack.1.near_hbm, f32[2304,128]{1,0:T(8,128)S(1)} %bitcast.10, bf16[256,64,128]{2,1,0:T(8,128)(2,1)} %left.2.lp_hbm, ...), custom_call_target="tpu_custom_call" | custom-call | flops 21849999360 | tf_op jit(solution)/shard_map/close/pallas_call | solution.py:314
  (1 shorter events, 0.0 us)
Async XLA Ops:
  1.9 19.9 %all-to-all-start = ((s32[16,1,256]{2,1,0:T(1,128)}), s32[16,1,256]{2,1,0:T(1,128)S(1)}, u32[]{:S(2)}, u32[]{:S(2)}) async-start(s32[16,1,256]{2,1,0:T(1,128)} %broadcast.3), calls=%async_computation | async-start | bytes 32768 | tf_op jit(solution)/shard_map/all_to_all | solution.py:457
  19.1 27.5 %collective-permute-start = (f32[18,48,128]{2,1,0:T(8,128)}, f32[18,48,128]{2,1,0:T(8,128)S(1)}, u32[]{:S(2)}, u32[]{:S(2)}) collective-permute-start(f32[18,48,128]{2,1,0:T(8,128)} %get-tuple-element.16.table_ref), channel_id=1, source_target_pairs={{0,16},{16,0},{1,17},{17,1},{2,18},{18,2},{3,19},{19,3},{4,20},{20... | collective-permute-start | bytes 1327112 | tf_op jit(solution)/shard_map/ppermute | solution.py:459
  21.8 1.0 %copy-start = (f32[18,48,128]{2,1,0:T(8,128)S(1)}, f32[18,48,128]{2,1,0:T(8,128)}, u32[]{:S(2)}) copy-start(f32[18,48,128]{2,1,0:T(8,128)} %get-tuple-element.16.table_ref) | copy-start | bytes 1327108
  24.4 31.2 %all-to-all-start.1 = ((f32[16,144,128]{2,1,0:T(8,128)}), f32[16,144,128]{2,1,0:T(8,128)S(1)}, u32[]{:S(2)}, u32[]{:S(2)}) async-start(f32[16,144,128]{2,1,0:T(8,128)} %bitcast.3), calls=%async_computation.1 | async-start | bytes 2359296 | tf_op jit(solution)/shard_map/all_to_all | solution.py:464
  55.6 14.4 %copy-start.4 = (f32[16,144,128]{2,1,0:T(8,128)}, f32[16,144,128]{2,1,0:T(8,128)S(1)}, u32[]{:S(2)}) copy-start(f32[16,144,128]{2,1,0:T(8,128)S(1)} %all-to-all-done.1) | copy-start | bytes 3538948
  55.6 21.4 %all-to-all-start.2 = ((f32[16,144,128]{2,1,0:T(8,128)}), f32[16,144,128]{2,1,0:T(8,128)S(1)}, u32[]{:S(2)}, u32[]{:S(2)}) async-start(f32[16,144,128]{2,1,0:T(8,128)} %bitcast.5), calls=%async_computation.2 | async-start | bytes 2359296 | tf_op jit(solution)/shard_map/all_to_all | solution.py:471
  70.0 7.0 %copy-start.1 = (s32[256]{0:T(256)S(1)}, s32[256]{0:T(256)}, u32[]{:S(2)}) copy-start(s32[256]{0:T(256)} %lslots_ref.1) | copy-start | bytes 3076
  70.0 7.0 %copy-start.2 = (s32[256]{0:T(256)S(1)}, s32[256]{0:T(256)}, u32[]{:S(2)}) copy-start(s32[256]{0:T(256)} %pslots_ref.1) | copy-start | bytes 3076
  70.0 7.0 %copy-start.3 = (s32[1,2]{1,0:T(1,128)S(1)}, s32[1,2]{1,0:T(1,128)}, u32[]{:S(2)}) copy-start(s32[1,2]{1,0:T(1,128)} %count_ref.1) | copy-start | bytes 28
